TPU v7x, 256 devices: a whole 4x4x8 slice. The times are simulated.
256 devices in a mesh: grp: 16 (over y, x), seq: 16 (over z, core).
Axes of the slice: x: 4, y: 4, z: 8, core: 2. Of those that a mesh axis runs over, the one named last changes fastest.
Arguments:
- queries: bfloat16 [16, 16, 512, 1536], P('grp', 'seq'), may hold values from -5 to 5
- keys: bfloat16 [16, 16, 512, 1536], P('grp', 'seq'), may hold values from -5 to 5
- values: bfloat16 [16, 16, 512, 1536], P('grp', 'seq'), may hold values from -5 to 5
- clip_frames: int32 [8, 4], replicated, may hold values from 1 to 8, 16 in all within a row
- clip_pixels: int32 [8, 4], replicated, may hold values from 256 to 1024
Outputs:
- attended: bfloat16 [16, 16, 512, 1536], P('grp', 'seq')
All inputs are finite; a program needn't handle non-finite values.
Results may differ from a plain program's by a relative error of at most 0.0051.
Values may be sent and summed in bfloat16 or wider, within the bound.
No kernel may reach another device: no remote copies, remote signals or barrier semaphores. Data moves between devices by JAX's collectives and lax.ppermute only.
A program may use at most 192 MiB of HBM per device.

v0:
```python
import functools

import jax
import jax.numpy as jnp
from jax import lax
from jax.experimental import pallas as pl
from jax.experimental.pallas import tpu as pltpu
from jax.sharding import PartitionSpec as P

DH = 128
CLIPS = 4
MASKED = -1e30
SCALE = DH**-0.5 * 1.4426950408889634
TBLOCK = 16
VMEM_LIMIT = 40 * 1024 * 1024


def scores_of(a, b):
    return lax.dot_general(a, b, (((1,), (1,)), ((), ())), preferred_element_type=jnp.float32)


def spatial_kernel(cf_ref, cp_ref, q_ref, k_ref, v_ref, fk_ref, fv_ref, o_ref):
    group_slot = lax.axis_index("grp")
    frame = lax.axis_index("seq")
    group = group_slot // 2
    half = group_slot % 2
    rows = q_ref.shape[0]
    limit = cp_ref[group, 0]
    end = cf_ref[group, 0]
    for clip in range(1, CLIPS):
        limit = jnp.where(frame >= end, cp_ref[group, clip], limit)
        end = end + cf_ref[group, clip]
    column = lax.broadcasted_iota(jnp.int32, (1, rows), 1)
    own_keep = column < limit - half * rows
    far_keep = column < limit - (1 - half) * rows
    for head in range(q_ref.shape[1] // DH):
        lanes = pl.ds(head * DH, DH)
        q = q_ref[:, lanes]
        own = jnp.where(own_keep, scores_of(q, k_ref[:, lanes]), MASKED)
        far = jnp.where(far_keep, scores_of(q, fk_ref[:, lanes]), MASKED)
        top = jnp.maximum(
            jnp.max(own, axis=1, keepdims=True), jnp.max(far, axis=1, keepdims=True)
        )
        own = jnp.exp2((own - top) * SCALE)
        far = jnp.exp2((far - top) * SCALE)
        total = jnp.sum(own, axis=1, keepdims=True) + jnp.sum(far, axis=1, keepdims=True)
        summed = jnp.dot(
            own.astype(jnp.bfloat16), v_ref[:, lanes], preferred_element_type=jnp.float32
        ) + jnp.dot(
            far.astype(jnp.bfloat16), fv_ref[:, lanes], preferred_element_type=jnp.float32
        )
        o_ref[:, lanes] = summed / total


def spatial_attention(clip_frames, clip_pixels, q, k, v, far_k, far_v):
    rows, width = q.shape
    heads = width // DH
    block = pl.BlockSpec((rows, DH), lambda h: (0, h))
    table = pl.BlockSpec(memory_space=pltpu.SMEM)
    return pl.pallas_call(
        spatial_kernel,
        grid=(heads,),
        in_specs=[table, table] + [block] * 5,
        out_specs=block,
        out_shape=jax.ShapeDtypeStruct((rows, width), jnp.float32),
        compiler_params=pltpu.CompilerParams(vmem_limit_bytes=VMEM_LIMIT),
        cost_estimate=pl.CostEstimate(
            flops=8 * rows * rows * width,
            bytes_accessed=rows * width * 14,
            transcendentals=2 * rows * rows * heads,
        ),
        name="spatial",
    )(clip_frames, clip_pixels, q, k, v, far_k, far_v)


def segment_of(frame, ends):
    return sum((frame >= end).astype(jnp.int32) for end in ends)


def temporal_kernel(cf_ref, qkv_ref, o_ref, keep_ref):
    frames, rows = o_ref.shape[0], o_ref.shape[1]
    size = frames * TBLOCK
    group = lax.axis_index("grp") // 2

    @pl.when(pl.program_id(0) == 0)
    def _():
        ends = []
        end = 0
        for clip in range(CLIPS):
            end = end + cf_ref[group, clip]
            ends.append(end)
        row = lax.broadcasted_iota(jnp.int32, (size, size), 0)
        col = lax.broadcasted_iota(jnp.int32, (size, size), 1)
        same_clip = segment_of(row // TBLOCK, ends) == segment_of(col // TBLOCK, ends)
        same_spot = row % TBLOCK == col % TBLOCK
        keep_ref[...] = jnp.where(same_clip & same_spot, 1.0, 0.0)

    keep = keep_ref[...] > 0.5
    for block in range(rows // TBLOCK):

        def part(which):
            at = pl.ds(which * rows + block * TBLOCK, TBLOCK)
            return qkv_ref[:, at, :].reshape(size, DH)

        scores = jnp.where(keep, scores_of(part(0), part(1)), MASKED)
        top = jnp.max(scores, axis=1, keepdims=True)
        weights = jnp.exp2((scores - top) * SCALE)
        total = jnp.sum(weights, axis=1, keepdims=True)
        summed = jnp.dot(weights.astype(jnp.bfloat16), part(2), preferred_element_type=jnp.float32)
        out = (summed / total).astype(o_ref.dtype)
        o_ref[:, pl.ds(block * TBLOCK, TBLOCK), :] = out.reshape(frames, TBLOCK, DH)


def temporal_attention(clip_frames, qkv):
    frames, rows3, width = qkv.shape
    rows = rows3 // 3
    heads = width // DH
    size = frames * TBLOCK
    return pl.pallas_call(
        temporal_kernel,
        grid=(heads,),
        in_specs=[
            pl.BlockSpec(memory_space=pltpu.SMEM),
            pl.BlockSpec((frames, rows3, DH), lambda h: (0, 0, h)),
        ],
        out_specs=pl.BlockSpec((frames, rows, DH), lambda h: (0, 0, h)),
        out_shape=jax.ShapeDtypeStruct((frames, rows, width), jnp.bfloat16),
        scratch_shapes=[pltpu.VMEM((size, size), jnp.float32)],
        compiler_params=pltpu.CompilerParams(vmem_limit_bytes=VMEM_LIMIT),
        cost_estimate=pl.CostEstimate(
            flops=4 * size * size * width * rows // TBLOCK,
            bytes_accessed=frames * rows * width * 8,
            transcendentals=size * size * heads * rows // TBLOCK,
        ),
        name="temporal",
    )(clip_frames, qkv)


def on_device(queries, keys, values, clip_frames, clip_pixels):
    rows, width = queries.shape[2], queries.shape[3]
    frames = lax.axis_size("seq")
    share = rows // frames
    q, k, v = queries[0, 0], keys[0, 0], values[0, 0]
    swap = [(i, i ^ 1) for i in range(lax.axis_size("grp"))]
    far_k = lax.ppermute(k, "grp", swap)
    far_v = lax.ppermute(v, "grp", swap)
    qkv = jnp.concatenate([x.reshape(frames, share, width) for x in (q, k, v)], axis=1)
    moved = lax.all_to_all(qkv, "seq", split_axis=0, concat_axis=0, tiled=True)
    temporal = temporal_attention(clip_frames, moved)
    spatial = spatial_attention(clip_frames, clip_pixels, q, k, v, far_k, far_v)
    back = lax.all_to_all(temporal, "seq", split_axis=0, concat_axis=0, tiled=True)
    attended = spatial + back.reshape(rows, width).astype(jnp.float32)
    return attended.astype(jnp.bfloat16)[None, None]


def solution(mesh):
    spec = P("grp", "seq", None, None)
    return jax.shard_map(
        on_device, mesh=mesh, in_specs=(spec, spec, spec, P(), P()), out_specs=spec, check_vma=False
    )
```

profile of v0, /device:TPU:1, one launch (start us, length us, event | category | flops | bytes accessed | tf_op | source)
XLA Modules:
  0.0 233.9 jit_solution(18378384555129487845)
XLA Ops:
  0.0 4.0 %pad_maximum_fusion = bf16[16,96,1536]{2,1,0:T(8,128)(2,1)} fusion(bf16[16,32,1536]{2,1,0:T(8,128)(2,1)} %bitcast.16, bf16[16,32,1536]{2,1,0:T(8,128)(2,1)} %bitcast.13, bf16[16,32,1536]{2,1,0:T(8,128)(2,1)} %bitcast.11), kind=kLoop, calls=%fused_computation | loop fusion | flops 14155776 | bytes 9437184 | tf_op jit(solution)/shard_map/concatenate | solution.py:147
  4.0 0.0 copy-start.5
  4.0 10.1 %all-to-all-start = ((bf16[16,96,1536]{2,1,0:T(8,128)(2,1)}), bf16[16,96,1536]{2,1,0:T(8,128)(2,1)}, u32[]{:S(2)}, u32[]{:S(2)}) async-start(bf16[16,96,1536]{2,1,0:T(8,128)(2,1)} %pad_maximum_fusion), calls=%async_computation | async-start | bytes 9437184 | tf_op jit(solution)/shard_map/all_to_all | solution.py:148
  14.1 0.0 copy-done.5
  14.1 0.1 copy.6.cf_ref
  14.2 104.7 %all-to-all-done.qkv_ref = bf16[16,96,1536]{2,1,0:T(8,128)(2,1)} async-done(((bf16[16,96,1536]{2,1,0:T(8,128)(2,1)}), bf16[16,96,1536]{2,1,0:T(8,128)(2,1)}, u32[]{:S(2)}, u32[]{:S(2)}) %all-to-all-start) | async-done | bytes 4718624 | tf_op jit(solution)/shard_map/all_to_all | solution.py:148
  118.9 12.2 %temporal.1 = bf16[16,32,1536]{2,1,0:T(8,128)(2,1)} custom-call(s32[8,4]{1,0:T(8,128)S(1)} %copy.6.cf_ref, bf16[16,96,1536]{2,1,0:T(8,128)(2,1)} %all-to-all-done.qkv_ref), custom_call_target="tpu_custom_call" | custom-call | flops 805306368 | bytes 6291456 | tf_op jit(solution)/shard_map/temporal/pallas_call | solution.py:119
  131.1 0.0 copy-start.1
  131.1 0.0 copy-start.3
  131.1 5.8 %all-to-all-start.1 = ((bf16[16,32,1536]{2,1,0:T(8,128)(2,1)}), bf16[16,32,1536]{2,1,0:T(8,128)(2,1)}, u32[]{:S(2)}, u32[]{:S(2)}) async-start(bf16[16,32,1536]{2,1,0:T(8,128)(2,1)} %temporal.1), calls=%async_computation.1 | async-start | bytes 3145728 | tf_op jit(solution)/shard_map/all_to_all | solution.py:151
  136.9 0.0 copy-done.1
  136.9 1.3 collective-permute-start
  138.2 0.0 copy-done.3
  138.2 0.3 collective-permute-start.1
  138.4 0.0 copy-done.6
  138.4 0.1 copy.7.cp_ref
  138.5 34.4 %collective-permute-done.fk_ref = bf16[512,1536]{1,0:T(8,128)(2,1)} collective-permute-done((bf16[512,1536]{1,0:T(8,128)(2,1)S(1)}, bf16[512,1536]{1,0:T(8,128)(2,1)}, u32[]{:S(2)}, u32[]{:S(2)}) %collective-permute-start) | collective-permute-done | bytes 1572896 | tf_op jit(solution)/shard_map/ppermute | solution.py:145
  172.9 33.7 %collective-permute-done.1.fv_ref = bf16[512,1536]{1,0:T(8,128)(2,1)} collective-permute-done((bf16[512,1536]{1,0:T(8,128)(2,1)S(1)}, bf16[512,1536]{1,0:T(8,128)(2,1)}, u32[]{:S(2)}, u32[]{:S(2)}) %collective-permute-start.1) | collective-permute-done | bytes 1572896 | tf_op jit(solution)/shard_map/ppermute | solution.py:146
  206.6 1.4 copy-done
  208.0 1.4 copy-done.2
  209.4 1.4 copy-done.4
  210.9 19.9 %spatial.1 = f32[512,1536]{1,0:T(8,128)S(1)} custom-call(s32[8,4]{1,0:T(8,128)S(1)} %copy.6.cf_ref, s32[8,4]{1,0:T(8,128)S(1)} %copy.7.cp_ref, bf16[512,1536]{1,0:T(8,128)(2,1)S(1)} %bitcast.12, bf16[512,1536]{1,0:T(8,128)(2,1)S(1)} %bitcast.15, bf16[512,1536]{1,0:T(8,128)(2,1)S(1)} %bitcast.18, bf16[512,1536]{1,0:T(8,128)(2,1)} %collective-permute-done.fk_ref, ...), custom_call_target="tpu_custom_call" | custom-call | flops 3221225472 | bytes 11010048 | tf_op jit(solution)/shard_map/spatial/pallas_call | solution.py:60
  230.7 0.0 all-to-all-done.1
  230.7 3.1 %fusion.1 = bf16[1,1,512,1536]{3,2,1,0:T(8,128)(2,1)} fusion(f32[512,1536]{1,0:T(8,128)S(1)} %spatial.1, bf16[16,32,1536]{2,1,0:T(8,128)(2,1)} %all-to-all-done.1), kind=kLoop, calls=%fused_computation.3 | loop fusion | flops 2359296 | bytes 6291456 | tf_op jit(solution)/shard_map/broadcast_in_dim | solution.py:153
  (4 shorter events, 0.0 us)
Async XLA Ops:
  4.0 10.1 %copy-start.5 = (s32[8,4]{0,1:T(4,128)S(1)}, s32[8,4]{0,1:T(4,128)}, u32[]{:S(2)}) copy-start(s32[8,4]{0,1:T(4,128)} %param.8) | copy-start | bytes 388
  4.0 115.0 %all-to-all-start = ((bf16[16,96,1536]{2,1,0:T(8,128)(2,1)}), bf16[16,96,1536]{2,1,0:T(8,128)(2,1)}, u32[]{:S(2)}, u32[]{:S(2)}) async-start(bf16[16,96,1536]{2,1,0:T(8,128)(2,1)} %pad_maximum_fusion), calls=%async_computation | async-start | bytes 9437184 | tf_op jit(solution)/shard_map/all_to_all | solution.py:148
  131.1 5.8 %copy-start.1 = (bf16[1,1,512,1536]{3,2,1,0:T(8,128)(2,1)S(1)}, bf16[1,1,512,1536]{3,2,1,0:T(8,128)(2,1)}, u32[]{:S(2)}) copy-start(bf16[1,1,512,1536]{3,2,1,0:T(8,128)(2,1)} %param.6) | copy-start | bytes 4718596
  131.1 7.1 %copy-start.3 = (bf16[1,1,512,1536]{3,2,1,0:T(8,128)(2,1)S(1)}, bf16[1,1,512,1536]{3,2,1,0:T(8,128)(2,1)}, u32[]{:S(2)}) copy-start(bf16[1,1,512,1536]{3,2,1,0:T(8,128)(2,1)} %param.7) | copy-start | bytes 4718596
  131.1 7.3 %copy-start.6 = (s32[8,4]{0,1:T(4,128)S(1)}, s32[8,4]{0,1:T(4,128)}, u32[]{:S(2)}) copy-start(s32[8,4]{0,1:T(4,128)} %param.9) | copy-start | bytes 388
  131.1 99.6 %all-to-all-start.1 = ((bf16[16,32,1536]{2,1,0:T(8,128)(2,1)}), bf16[16,32,1536]{2,1,0:T(8,128)(2,1)}, u32[]{:S(2)}, u32[]{:S(2)}) async-start(bf16[16,32,1536]{2,1,0:T(8,128)(2,1)} %temporal.1), calls=%async_computation.1 | async-start | bytes 3145728 | tf_op jit(solution)/shard_map/all_to_all | solution.py:151
  136.9 36.0 %collective-permute-start = (bf16[512,1536]{1,0:T(8,128)(2,1)S(1)}, bf16[512,1536]{1,0:T(8,128)(2,1)}, u32[]{:S(2)}, u32[]{:S(2)}) collective-permute-start(bf16[512,1536]{1,0:T(8,128)(2,1)S(1)} %bitcast.14), channel_id=1, source_target_pairs={{0,16},{16,0},{32,48},{48,32},{64,80},{80,64},{96,112},{112,96},{1... | collective-permute-start | bytes 4718600 | tf_op jit(solution)/shard_map/ppermute | solution.py:145
  138.2 68.4 %collective-permute-start.1 = (bf16[512,1536]{1,0:T(8,128)(2,1)S(1)}, bf16[512,1536]{1,0:T(8,128)(2,1)}, u32[]{:S(2)}, u32[]{:S(2)}) collective-permute-start(bf16[512,1536]{1,0:T(8,128)(2,1)S(1)} %bitcast.17), channel_id=1, source_target_pairs={{0,16},{16,0},{32,48},{48,32},{64,80},{80,64},{96,112},{112,96},{1... | collective-permute-start | bytes 4718600 | tf_op jit(solution)/shard_map/ppermute | solution.py:146
  206.6 1.4 copy-start
  208.0 1.4 copy-start.2
  209.4 1.4 copy-start.4
where the time goes:
time: 234 us
  waiting for transfers between devices  173 us (74%)
  Pallas kernels  32.1 us (14%)
  starting transfers between devices  17.4 us (7%)
  other arithmetic  7.09 us (3%)
  local copies, waits for them, and re-layouts  4.4 us (2%)
    all_to_all x1, waiting for transfers between devices, on_device(): moved = lax.all_to_all(qkv, 'seq', split_axis=0, concat_axis=0, tiled=True)  105 us
    ppermute x1, waiting for transfers between devices, on_device(): far_k = lax.ppermute(k, 'grp', swap)  34.4 us
    ppermute x1, waiting for transfers between devices, on_device(): far_v = lax.ppermute(v, 'grp', swap)  33.7 us
    pallas_call x1, Pallas kernels, spatial_attention(): pl.pallas_call(spatial_kernel, grid=(heads,), in_specs=[table, table] + [...  19.9 us
    pallas_call x1, Pallas kernels, temporal_attention(): pl.pallas_call(temporal_kernel, grid=(heads,), in_specs=[pl.BlockSpec(mem...  12.2 us
    all_to_all x1, starting transfers between devices, on_device(): moved = lax.all_to_all(qkv, 'seq', split_axis=0, concat_axis=0, tiled=True)  10.1 us
    all_to_all x1, starting transfers between devices, on_device(): lax.all_to_all(temporal, 'seq', split_axis=0, concat_axis=0, tiled=True)  5.76 us
  transfers between devices with their start and end apart: 4, of which 3 were waited for; matrix products, arithmetic and copies ran while one was open for 0% of the time, Pallas kernels for 8%

commit v1 on v0

v1 whole, which is shorter than its diff:
```python
import jax
import jax.numpy as jnp
from jax import lax
from jax.experimental import pallas as pl
from jax.experimental.pallas import tpu as pltpu
from jax.sharding import PartitionSpec as P

DH = 128
CLIPS = 4
MASKED = -1e30
SCALE = DH**-0.5 * 1.4426950408889634
TBLOCK = 16
PARAMS = pltpu.CompilerParams(vmem_limit_bytes=24 * 1024 * 1024)
SMEM = pl.BlockSpec(memory_space=pltpu.SMEM)


def scores_of(a, b):
    return lax.dot_general(a, b, (((1,), (1,)), ((), ())), preferred_element_type=jnp.float32)


def product(a, b):
    return jnp.dot(a, b, preferred_element_type=jnp.float32)


def spatial_kernel(cf_ref, cp_ref, q_ref, k_ref, v_ref, fk_ref, fv_ref, o_ref):
    group_slot = lax.axis_index("grp")
    frame = lax.axis_index("seq")
    group = group_slot // 2
    half = group_slot % 2
    rows = q_ref.shape[0]
    limit = cp_ref[group, 0]
    end = cf_ref[group, 0]
    for clip in range(1, CLIPS):
        limit = jnp.where(frame >= end, cp_ref[group, clip], limit)
        end = end + cf_ref[group, clip]
    column = lax.broadcasted_iota(jnp.int32, (1, rows), 1)
    own_keep = column < limit - half * rows
    far_keep = column < limit - (1 - half) * rows
    for head in range(q_ref.shape[1] // DH):
        lanes = pl.ds(head * DH, DH)
        q = q_ref[:, lanes]
        own = jnp.where(own_keep, scores_of(q, k_ref[:, lanes]), MASKED)
        far = jnp.where(far_keep, scores_of(q, fk_ref[:, lanes]), MASKED)
        top = jnp.maximum(
            jnp.max(own, axis=1, keepdims=True), jnp.max(far, axis=1, keepdims=True)
        )
        own = jnp.exp2((own - top) * SCALE)
        far = jnp.exp2((far - top) * SCALE)
        total = jnp.sum(own, axis=1, keepdims=True) + jnp.sum(far, axis=1, keepdims=True)
        summed = product(own.astype(jnp.bfloat16), v_ref[:, lanes])
        summed = summed + product(far.astype(jnp.bfloat16), fv_ref[:, lanes])
        o_ref[:, lanes] = summed / total


def spatial_attention(clip_frames, clip_pixels, q, k, v, far_k, far_v, start):
    rows, width = far_k.shape
    heads = width // DH
    block = pl.BlockSpec((rows, DH), lambda h: (0, h))
    whole = pl.BlockSpec((rows, DH), lambda h: (0, h + start // DH))
    return pl.pallas_call(
        spatial_kernel,
        grid=(heads,),
        in_specs=[SMEM, SMEM, whole, whole, whole, block, block],
        out_specs=block,
        out_shape=jax.ShapeDtypeStruct((rows, width), jnp.float32),
        compiler_params=PARAMS,
        cost_estimate=pl.CostEstimate(
            flops=8 * rows * rows * width,
            bytes_accessed=rows * width * 14,
            transcendentals=2 * rows * rows * heads,
        ),
        name="spatial",
    )(clip_frames, clip_pixels, q, k, v, far_k, far_v)


def clip_mask(cf_ref, keep_ref, frames, rolled):
    size = keep_ref.shape[0]
    group = lax.axis_index("grp") // 2
    me = lax.axis_index("seq")
    row = lax.broadcasted_iota(jnp.int32, (size, size), 0)
    col = lax.broadcasted_iota(jnp.int32, (size, size), 1)
    same_spot = row % TBLOCK == col % TBLOCK

    def frame_of(index):
        slot = index // TBLOCK
        if not rolled:
            return slot
        return (me + frames - slot) % frames

    def segment_of(index):
        frame = frame_of(index)
        end = 0
        segment = jnp.zeros_like(frame)
        for clip in range(CLIPS):
            end = end + cf_ref[group, clip]
            segment = segment + (frame >= end).astype(jnp.int32)
        return segment

    keep = same_spot & (segment_of(row) == segment_of(col))
    keep_ref[...] = jnp.where(keep, 0.0, MASKED)


def temporal_block(bias, q, k, v):
    scores = scores_of(q, k) + bias
    top = jnp.max(scores, axis=1, keepdims=True)
    weights = jnp.exp2((scores - top) * SCALE)
    total = jnp.sum(weights, axis=1, keepdims=True)
    return (product(weights.astype(jnp.bfloat16), v) / total).astype(jnp.bfloat16)


def temporal_kernel(cf_ref, qkv_ref, o_ref, keep_ref):
    frames, rows, width = o_ref.shape
    size = frames * TBLOCK

    @pl.when(pl.program_id(0) == 0)
    def _():
        clip_mask(cf_ref, keep_ref, frames, False)

    bias = keep_ref[...]
    for head in range(width // DH):
        lanes = pl.ds(head * DH, DH)
        for block in range(rows // TBLOCK):
            q, k, v = (
                qkv_ref[:, pl.ds(which * rows + block * TBLOCK, TBLOCK), lanes].reshape(size, DH)
                for which in range(3)
            )
            out = temporal_block(bias, q, k, v)
            o_ref[:, pl.ds(block * TBLOCK, TBLOCK), lanes] = out.reshape(frames, TBLOCK, DH)


def temporal_cost(frames, rows, width):
    size = frames * TBLOCK
    return pl.CostEstimate(
        flops=4 * size * size * width * rows // TBLOCK,
        bytes_accessed=frames * rows * width * 8,
        transcendentals=size * size * (width // DH) * rows // TBLOCK,
    )


def temporal_attention(clip_frames, qkv, heads_step):
    frames, rows3, width = qkv.shape
    rows = rows3 // 3
    lanes = heads_step * DH
    size = frames * TBLOCK
    return pl.pallas_call(
        temporal_kernel,
        grid=(width // lanes,),
        in_specs=[SMEM, pl.BlockSpec((frames, rows3, lanes), lambda h: (0, 0, h))],
        out_specs=pl.BlockSpec((frames, rows, lanes), lambda h: (0, 0, h)),
        out_shape=jax.ShapeDtypeStruct((frames, rows, width), jnp.bfloat16),
        scratch_shapes=[pltpu.VMEM((size, size), jnp.float32)],
        compiler_params=PARAMS,
        cost_estimate=temporal_cost(frames, rows, width),
        name="temporal",
    )(clip_frames, qkv)


def all_to_all(array):
    return lax.all_to_all(array, "seq", split_axis=0, concat_axis=0, tiled=True)


def on_device(queries, keys, values, clip_frames, clip_pixels):
    rows, width = queries.shape[2], queries.shape[3]
    frames = lax.axis_size("seq")
    q, k, v = queries[0, 0], keys[0, 0], values[0, 0]
    swap = [(i, i ^ 1) for i in range(lax.axis_size("grp"))]
    packed = jnp.concatenate([x.reshape(frames, rows // frames, width) for x in (q, k, v)], axis=1)
    moved = all_to_all(packed)
    far_k = lax.ppermute(k, "grp", swap)
    far_v = lax.ppermute(v, "grp", swap)
    spatial = spatial_attention(clip_frames, clip_pixels, q, k, v, far_k, far_v, 0)
    moved, spatial = lax.optimization_barrier((moved, spatial))
    back = all_to_all(temporal_attention(clip_frames, moved, 4))
    attended = spatial + back.reshape(rows, width).astype(jnp.float32)
    return attended.astype(jnp.bfloat16)[None, None]


def solution(mesh):
    spec = P("grp", "seq", None, None)
    return jax.shard_map(
        on_device, mesh=mesh, in_specs=(spec, spec, spec, P(), P()), out_specs=spec, check_vma=False
    )
```

time: 234 us -> 171 us (0.73)
  waiting for transfers between devices: 173 us -> 79 us
  blocking collectives: 0 us -> 45.1 us
  Pallas kernels: 32.1 us -> 25.2 us
  starting transfers between devices: 17.4 us -> 11.8 us
    all_to_all x2 -> x1, waiting for transfers between devices: 105 us -> 11 us  [all_to_all(): return lax.all_to_all(array, 'seq', split_axis=0, concat_axis=0, tiled=True)]
    all_to_all x0 -> x1, blocking collectives: none -> 45.1 us  [all_to_all(): return lax.all_to_all(array, 'seq', split_axis=0, concat_axis=0, tiled=True)]
    pallas_call x2, Pallas kernels: 32.1 us -> 25.2 us  [the longest x1 19.9 us: spatial_attention(): pl.pallas_call(spatial_kernel, grid=(heads,), in_specs=[SMEM, SMEM, whole...]
    all_to_all x2 -> x1, starting transfers between devices: 15.9 us -> 10.3 us  [all_to_all(): return lax.all_to_all(array, 'seq', split_axis=0, concat_axis=0, tiled=True)]
  transfers between devices with their start and end apart: 4 -> 3, of which waited for: 3 -> 3; matrix products, arithmetic and copies ran while one was open for 0% -> 0% of each run, Pallas kernels for 8% -> 12%
where the time goes in v1:
time: 171 us
  waiting for transfers between devices  79 us (46%)
  blocking collectives  45.1 us (26%)
  Pallas kernels  25.2 us (15%)
  starting transfers between devices  11.8 us (7%)
  other arithmetic  5.67 us (3%)
  local copies, waits for them, and re-layouts  4.4 us (3%)
    all_to_all x1, blocking collectives, all_to_all(): return lax.all_to_all(array, 'seq', split_axis=0, concat_axis=0, tiled=True)  45.1 us
    ppermute x1, waiting for transfers between devices, on_device(): far_k = lax.ppermute(k, 'grp', swap)  34.3 us
    ppermute x1, waiting for transfers between devices, on_device(): far_v = lax.ppermute(v, 'grp', swap)  33.7 us
    pallas_call x1, Pallas kernels, spatial_attention(): pl.pallas_call(spatial_kernel, grid=(heads,), in_specs=[SMEM, SMEM, whole...  19.9 us
    all_to_all x1, waiting for transfers between devices, all_to_all(): return lax.all_to_all(array, 'seq', split_axis=0, concat_axis=0, tiled=True)  11 us
    all_to_all x1, starting transfers between devices, all_to_all(): return lax.all_to_all(array, 'seq', split_axis=0, concat_axis=0, tiled=True)  10.3 us
    pallas_call x1, Pallas kernels, temporal_attention(): pl.pallas_call(temporal_kernel, grid=(width // lanes,), in_specs=[SMEM, p...  5.29 us
    unnamed x16, local copies, waits for them, and re-layouts  4.4 us
  transfers between devices with their start and end apart: 3, of which 3 were waited for; matrix products, arithmetic and copies ran while one was open for 0% of the time, Pallas kernels for 12%

profile of v1, /device:TPU:1, one launch (start us, length us, event | category | flops | bytes accessed | tf_op | source)
XLA Modules:
  0.0 171.2 jit_solution(8063877029565260605)
XLA Ops:
  0.0 4.0 %pad_maximum_fusion = bf16[16,96,1536]{2,1,0:T(8,128)(2,1)} fusion(bf16[16,32,1536]{2,1,0:T(8,128)(2,1)} %bitcast.16, bf16[16,32,1536]{2,1,0:T(8,128)(2,1)} %bitcast.13, bf16[16,32,1536]{2,1,0:T(8,128)(2,1)} %bitcast.11), kind=kLoop, calls=%fused_computation | loop fusion | flops 14155776 | bytes 9437184 | tf_op jit(solution)/shard_map/concatenate | solution.py:167
  4.0 0.0 copy-start.1
  4.0 0.0 copy-start.3
  4.0 0.0 copy-start.5
  4.0 0.0 copy-start.6
  4.0 10.3 %all-to-all-start = ((bf16[16,96,1536]{2,1,0:T(8,128)(2,1)}), bf16[16,96,1536]{2,1,0:T(8,128)(2,1)}, u32[]{:S(2)}, u32[]{:S(2)}) async-start(bf16[16,96,1536]{2,1,0:T(8,128)(2,1)} %pad_maximum_fusion), calls=%async_computation | async-start | bytes 9437184 | tf_op jit(solution)/shard_map/all_to_all | solution.py:159
  14.2 0.0 copy-done.1
  14.3 1.3 collective-permute-start
  15.6 0.0 copy-done.3
  15.6 0.3 collective-permute-start.1
  15.8 0.0 copy-done.5
  15.8 0.1 copy.6.cf_ref
  15.9 0.0 copy-done.6
  15.9 0.1 copy.7.cp_ref
  16.0 34.3 %collective-permute-done.fk_ref = bf16[512,1536]{1,0:T(8,128)(2,1)} collective-permute-done((bf16[512,1536]{1,0:T(8,128)(2,1)S(1)}, bf16[512,1536]{1,0:T(8,128)(2,1)}, u32[]{:S(2)}, u32[]{:S(2)}) %collective-permute-start) | collective-permute-done | bytes 1572896 | tf_op jit(solution)/shard_map/ppermute | solution.py:169
  50.3 33.7 %collective-permute-done.1.fv_ref = bf16[512,1536]{1,0:T(8,128)(2,1)} collective-permute-done((bf16[512,1536]{1,0:T(8,128)(2,1)S(1)}, bf16[512,1536]{1,0:T(8,128)(2,1)}, u32[]{:S(2)}, u32[]{:S(2)}) %collective-permute-start.1) | collective-permute-done | bytes 1572896 | tf_op jit(solution)/shard_map/ppermute | solution.py:170
  84.0 1.4 copy-done
  85.4 1.4 copy-done.2
  86.8 1.4 copy-done.4
  88.2 19.9 %spatial.1 = f32[512,1536]{1,0:T(8,128)S(1)} custom-call(s32[8,4]{1,0:T(8,128)S(1)} %copy.6.cf_ref, s32[8,4]{1,0:T(8,128)S(1)} %copy.7.cp_ref, bf16[512,1536]{1,0:T(8,128)(2,1)S(1)} %bitcast.12, bf16[512,1536]{1,0:T(8,128)(2,1)S(1)} %bitcast.15, bf16[512,1536]{1,0:T(8,128)(2,1)S(1)} %bitcast.18, bf16[512,1536]{1,0:T(8,128)(2,1)} %collective-permute-done.fk_ref, ...), custom_call_target="tpu_custom_call" | custom-call | flops 3221225472 | bytes 11010048 | tf_op jit(solution)/shard_map/spatial/pallas_call | solution.py:60
  108.1 11.0 %all-to-all-done.qkv_ref = bf16[16,96,1536]{2,1,0:T(8,128)(2,1)} async-done(((bf16[16,96,1536]{2,1,0:T(8,128)(2,1)}), bf16[16,96,1536]{2,1,0:T(8,128)(2,1)}, u32[]{:S(2)}, u32[]{:S(2)}) %all-to-all-start) | async-done | bytes 4718624 | tf_op jit(solution)/shard_map/all_to_all | solution.py:159
  119.1 5.3 %temporal.1 = bf16[16,32,1536]{2,1,0:T(8,128)(2,1)S(1)} custom-call(s32[8,4]{1,0:T(8,128)S(1)} %copy.6.cf_ref, bf16[16,96,1536]{2,1,0:T(8,128)(2,1)} %all-to-all-done.qkv_ref), custom_call_target="tpu_custom_call" | custom-call | flops 805306368 | bytes 6291456 | tf_op jit(solution)/shard_map/temporal/pallas_call | solution.py:145
  124.4 45.1 %all_to_all.10 = bf16[16,32,1536]{2,1,0:T(8,128)(2,1)S(1)} all-to-all(bf16[16,32,1536]{2,1,0:T(8,128)(2,1)S(1)} %temporal.1), channel_id=1, replica_groups=mesh['grp'=16,'seq'=16] {'seq'}, dimensions={0} | all-to-all | bytes 3145728 | tf_op jit(solution)/shard_map/all_to_all | solution.py:159
  169.4 1.7 fusion.1
  (3 shorter events, 0.0 us)
Async XLA Ops:
  4.0 10.3 %copy-start.1 = (bf16[1,1,512,1536]{3,2,1,0:T(8,128)(2,1)S(1)}, bf16[1,1,512,1536]{3,2,1,0:T(8,128)(2,1)}, u32[]{:S(2)}) copy-start(bf16[1,1,512,1536]{3,2,1,0:T(8,128)(2,1)} %param.6) | copy-start | bytes 4718596
  4.0 11.6 %copy-start.3 = (bf16[1,1,512,1536]{3,2,1,0:T(8,128)(2,1)S(1)}, bf16[1,1,512,1536]{3,2,1,0:T(8,128)(2,1)}, u32[]{:S(2)}) copy-start(bf16[1,1,512,1536]{3,2,1,0:T(8,128)(2,1)} %param.7) | copy-start | bytes 4718596
  4.0 11.8 %copy-start.5 = (s32[8,4]{0,1:T(4,128)S(1)}, s32[8,4]{0,1:T(4,128)}, u32[]{:S(2)}) copy-start(s32[8,4]{0,1:T(4,128)} %param.8) | copy-start | bytes 388
  4.0 11.9 %copy-start.6 = (s32[8,4]{0,1:T(4,128)S(1)}, s32[8,4]{0,1:T(4,128)}, u32[]{:S(2)}) copy-start(s32[8,4]{0,1:T(4,128)} %param.9) | copy-start | bytes 388
  4.0 115.1 %all-to-all-start = ((bf16[16,96,1536]{2,1,0:T(8,128)(2,1)}), bf16[16,96,1536]{2,1,0:T(8,128)(2,1)}, u32[]{:S(2)}, u32[]{:S(2)}) async-start(bf16[16,96,1536]{2,1,0:T(8,128)(2,1)} %pad_maximum_fusion), calls=%async_computation | async-start | bytes 9437184 | tf_op jit(solution)/shard_map/all_to_all | solution.py:159
  14.3 36.0 %collective-permute-start = (bf16[512,1536]{1,0:T(8,128)(2,1)S(1)}, bf16[512,1536]{1,0:T(8,128)(2,1)}, u32[]{:S(2)}, u32[]{:S(2)}) collective-permute-start(bf16[512,1536]{1,0:T(8,128)(2,1)S(1)} %bitcast.14), channel_id=1, source_target_pairs={{0,16},{16,0},{32,48},{48,32},{64,80},{80,64},{96,112},{112,96},{1... | collective-permute-start | bytes 4718600 | tf_op jit(solution)/shard_map/ppermute | solution.py:169
  15.6 68.4 %collective-permute-start.1 = (bf16[512,1536]{1,0:T(8,128)(2,1)S(1)}, bf16[512,1536]{1,0:T(8,128)(2,1)}, u32[]{:S(2)}, u32[]{:S(2)}) collective-permute-start(bf16[512,1536]{1,0:T(8,128)(2,1)S(1)} %bitcast.17), channel_id=1, source_target_pairs={{0,16},{16,0},{32,48},{48,32},{64,80},{80,64},{96,112},{112,96},{1... | collective-permute-start | bytes 4718600 | tf_op jit(solution)/shard_map/ppermute | solution.py:170
  84.0 1.4 copy-start
  85.4 1.4 copy-start.2
  86.8 1.4 copy-start.4

commit v2 on v1

--- a/solution.py
+++ b/solution.py
@@ -103,9 +103,9 @@
 def temporal_block(bias, q, k, v):
     scores = scores_of(q, k) + bias
     top = jnp.max(scores, axis=1, keepdims=True)
-    weights = jnp.exp2((scores - top) * SCALE)
-    total = jnp.sum(weights, axis=1, keepdims=True)
-    return (product(weights.astype(jnp.bfloat16), v) / total).astype(jnp.bfloat16)
+    weights = jnp.exp2((scores - top) * SCALE).astype(jnp.bfloat16)
+    summed = product(weights, jnp.concatenate([v, jnp.ones_like(v)], axis=1))
+    return (summed[:, :DH] / summed[:, DH:]).astype(jnp.bfloat16)
 
 
 def temporal_kernel(cf_ref, qkv_ref, o_ref, keep_ref):
@@ -170,7 +170,7 @@
     far_v = lax.ppermute(v, "grp", swap)
     spatial = spatial_attention(clip_frames, clip_pixels, q, k, v, far_k, far_v, 0)
     moved, spatial = lax.optimization_barrier((moved, spatial))
-    back = all_to_all(temporal_attention(clip_frames, moved, 4))
+    back = all_to_all(temporal_attention(clip_frames, moved, 6))
     attended = spatial + back.reshape(rows, width).astype(jnp.float32)
     return attended.astype(jnp.bfloat16)[None, None]
 

time: 171 us -> 170 us (level)
  no operation moved by 1% of the time
where the time goes in v2:
time: 170 us
  waiting for transfers between devices  79 us (46%)
  blocking collectives  45.1 us (27%)
  Pallas kernels  24.1 us (14%)
  starting transfers between devices  11.8 us (7%)
  other arithmetic  5.67 us (3%)
  local copies, waits for them, and re-layouts  4.4 us (3%)
    all_to_all x1, blocking collectives, all_to_all(): return lax.all_to_all(array, 'seq', split_axis=0, concat_axis=0, tiled=True)  45.1 us
    ppermute x1, waiting for transfers between devices, on_device(): far_k = lax.ppermute(k, 'grp', swap)  34.3 us
    ppermute x1, waiting for transfers between devices, on_device(): far_v = lax.ppermute(v, 'grp', swap)  33.7 us
    pallas_call x1, Pallas kernels, spatial_attention(): pl.pallas_call(spatial_kernel, grid=(heads,), in_specs=[SMEM, SMEM, whole...  19.9 us
    all_to_all x1, waiting for transfers between devices, all_to_all(): return lax.all_to_all(array, 'seq', split_axis=0, concat_axis=0, tiled=True)  11 us
    all_to_all x1, starting transfers between devices, all_to_all(): return lax.all_to_all(array, 'seq', split_axis=0, concat_axis=0, tiled=True)  10.3 us
    unnamed x16, local copies, waits for them, and re-layouts  4.4 us
    pallas_call x1, Pallas kernels, temporal_attention(): pl.pallas_call(temporal_kernel, grid=(width // lanes,), in_specs=[SMEM, p...  4.25 us
  transfers between devices with their start and end apart: 3, of which 3 were waited for; matrix products, arithmetic and copies ran while one was open for 0% of the time, Pallas kernels for 12%

profile of v2, /device:TPU:1, one launch (start us, length us, event | category | flops | bytes accessed | tf_op | source)
XLA Modules:
  0.0 170.1 jit_solution(15584409350890507139)
XLA Ops:
  0.0 4.0 %pad_maximum_fusion = bf16[16,96,1536]{2,1,0:T(8,128)(2,1)} fusion(bf16[16,32,1536]{2,1,0:T(8,128)(2,1)} %bitcast.16, bf16[16,32,1536]{2,1,0:T(8,128)(2,1)} %bitcast.13, bf16[16,32,1536]{2,1,0:T(8,128)(2,1)} %bitcast.11), kind=kLoop, calls=%fused_computation | loop fusion | flops 14155776 | bytes 9437184 | tf_op jit(solution)/shard_map/concatenate | solution.py:167
  4.0 0.0 copy-start.1
  4.0 0.0 copy-start.3
  4.0 0.0 copy-start.5
  4.0 0.0 copy-start.6
  4.0 10.3 %all-to-all-start = ((bf16[16,96,1536]{2,1,0:T(8,128)(2,1)}), bf16[16,96,1536]{2,1,0:T(8,128)(2,1)}, u32[]{:S(2)}, u32[]{:S(2)}) async-start(bf16[16,96,1536]{2,1,0:T(8,128)(2,1)} %pad_maximum_fusion), calls=%async_computation | async-start | bytes 9437184 | tf_op jit(solution)/shard_map/all_to_all | solution.py:159
  14.2 0.0 copy-done.1
  14.3 1.3 collective-permute-start
  15.6 0.0 copy-done.3
  15.6 0.3 collective-permute-start.1
  15.8 0.0 copy-done.5
  15.8 0.1 copy.6.cf_ref
  15.9 0.0 copy-done.6
  15.9 0.1 copy.7.cp_ref
  16.0 34.3 %collective-permute-done.fk_ref = bf16[512,1536]{1,0:T(8,128)(2,1)} collective-permute-done((bf16[512,1536]{1,0:T(8,128)(2,1)S(1)}, bf16[512,1536]{1,0:T(8,128)(2,1)}, u32[]{:S(2)}, u32[]{:S(2)}) %collective-permute-start) | collective-permute-done | bytes 1572896 | tf_op jit(solution)/shard_map/ppermute | solution.py:169
  50.3 33.7 %collective-permute-done.1.fv_ref = bf16[512,1536]{1,0:T(8,128)(2,1)} collective-permute-done((bf16[512,1536]{1,0:T(8,128)(2,1)S(1)}, bf16[512,1536]{1,0:T(8,128)(2,1)}, u32[]{:S(2)}, u32[]{:S(2)}) %collective-permute-start.1) | collective-permute-done | bytes 1572896 | tf_op jit(solution)/shard_map/ppermute | solution.py:170
  84.0 1.4 copy-done
  85.4 1.4 copy-done.2
  86.8 1.4 copy-done.4
  88.2 19.9 %spatial.1 = f32[512,1536]{1,0:T(8,128)S(1)} custom-call(s32[8,4]{1,0:T(8,128)S(1)} %copy.6.cf_ref, s32[8,4]{1,0:T(8,128)S(1)} %copy.7.cp_ref, bf16[512,1536]{1,0:T(8,128)(2,1)S(1)} %bitcast.12, bf16[512,1536]{1,0:T(8,128)(2,1)S(1)} %bitcast.15, bf16[512,1536]{1,0:T(8,128)(2,1)S(1)} %bitcast.18, bf16[512,1536]{1,0:T(8,128)(2,1)} %collective-permute-done.fk_ref, ...), custom_call_target="tpu_custom_call" | custom-call | flops 3221225472 | bytes 11010048 | tf_op jit(solution)/shard_map/spatial/pallas_call | solution.py:60
  108.1 11.0 %all-to-all-done.qkv_ref = bf16[16,96,1536]{2,1,0:T(8,128)(2,1)} async-done(((bf16[16,96,1536]{2,1,0:T(8,128)(2,1)}), bf16[16,96,1536]{2,1,0:T(8,128)(2,1)}, u32[]{:S(2)}, u32[]{:S(2)}) %all-to-all-start) | async-done | bytes 4718624 | tf_op jit(solution)/shard_map/all_to_all | solution.py:159
  119.1 4.2 %temporal.1 = bf16[16,32,1536]{2,1,0:T(8,128)(2,1)S(1)} custom-call(s32[8,4]{1,0:T(8,128)S(1)} %copy.6.cf_ref, bf16[16,96,1536]{2,1,0:T(8,128)(2,1)} %all-to-all-done.qkv_ref), custom_call_target="tpu_custom_call" | custom-call | flops 805306368 | bytes 6291456 | tf_op jit(solution)/shard_map/temporal/pallas_call | solution.py:145
  123.3 45.1 %all_to_all.10 = bf16[16,32,1536]{2,1,0:T(8,128)(2,1)S(1)} all-to-all(bf16[16,32,1536]{2,1,0:T(8,128)(2,1)S(1)} %temporal.1), channel_id=1, replica_groups=mesh['grp'=16,'seq'=16] {'seq'}, dimensions={0} | all-to-all | bytes 3145728 | tf_op jit(solution)/shard_map/all_to_all | solution.py:159
  168.4 1.7 fusion.1
  (3 shorter events, 0.0 us)
Async XLA Ops:
  4.0 10.3 %copy-start.1 = (bf16[1,1,512,1536]{3,2,1,0:T(8,128)(2,1)S(1)}, bf16[1,1,512,1536]{3,2,1,0:T(8,128)(2,1)}, u32[]{:S(2)}) copy-start(bf16[1,1,512,1536]{3,2,1,0:T(8,128)(2,1)} %param.6) | copy-start | bytes 4718596
  4.0 11.6 %copy-start.3 = (bf16[1,1,512,1536]{3,2,1,0:T(8,128)(2,1)S(1)}, bf16[1,1,512,1536]{3,2,1,0:T(8,128)(2,1)}, u32[]{:S(2)}) copy-start(bf16[1,1,512,1536]{3,2,1,0:T(8,128)(2,1)} %param.7) | copy-start | bytes 4718596
  4.0 11.8 %copy-start.5 = (s32[8,4]{0,1:T(4,128)S(1)}, s32[8,4]{0,1:T(4,128)}, u32[]{:S(2)}) copy-start(s32[8,4]{0,1:T(4,128)} %param.8) | copy-start | bytes 388
  4.0 11.9 %copy-start.6 = (s32[8,4]{0,1:T(4,128)S(1)}, s32[8,4]{0,1:T(4,128)}, u32[]{:S(2)}) copy-start(s32[8,4]{0,1:T(4,128)} %param.9) | copy-start | bytes 388
  4.0 115.1 %all-to-all-start = ((bf16[16,96,1536]{2,1,0:T(8,128)(2,1)}), bf16[16,96,1536]{2,1,0:T(8,128)(2,1)}, u32[]{:S(2)}, u32[]{:S(2)}) async-start(bf16[16,96,1536]{2,1,0:T(8,128)(2,1)} %pad_maximum_fusion), calls=%async_computation | async-start | bytes 9437184 | tf_op jit(solution)/shard_map/all_to_all | solution.py:159
  14.3 36.0 %collective-permute-start = (bf16[512,1536]{1,0:T(8,128)(2,1)S(1)}, bf16[512,1536]{1,0:T(8,128)(2,1)}, u32[]{:S(2)}, u32[]{:S(2)}) collective-permute-start(bf16[512,1536]{1,0:T(8,128)(2,1)S(1)} %bitcast.14), channel_id=1, source_target_pairs={{0,16},{16,0},{32,48},{48,32},{64,80},{80,64},{96,112},{112,96},{1... | collective-permute-start | bytes 4718600 | tf_op jit(solution)/shard_map/ppermute | solution.py:169
  15.6 68.4 %collective-permute-start.1 = (bf16[512,1536]{1,0:T(8,128)(2,1)S(1)}, bf16[512,1536]{1,0:T(8,128)(2,1)}, u32[]{:S(2)}, u32[]{:S(2)}) collective-permute-start(bf16[512,1536]{1,0:T(8,128)(2,1)S(1)} %bitcast.17), channel_id=1, source_target_pairs={{0,16},{16,0},{32,48},{48,32},{64,80},{80,64},{96,112},{112,96},{1... | collective-permute-start | bytes 4718600 | tf_op jit(solution)/shard_map/ppermute | solution.py:170
  84.0 1.4 copy-start
  85.4 1.4 copy-start.2
  86.8 1.4 copy-start.4

commit v3 on v2

--- a/solution.py
+++ b/solution.py
@@ -1,3 +1,5 @@
+import functools
+
 import jax
 import jax.numpy as jnp
 from jax import lax
@@ -10,7 +12,10 @@
 MASKED = -1e30
 SCALE = DH**-0.5 * 1.4426950408889634
 TBLOCK = 16
+SHIFTS = (7, 9, 6, 10, 5, 11, 8, 4, 12, 3, 13, 2, 14, 1, 15)
+SLOTS = SHIFTS + (0,)
 PARAMS = pltpu.CompilerParams(vmem_limit_bytes=24 * 1024 * 1024)
+WIDE = pltpu.CompilerParams(vmem_limit_bytes=60 * 1024 * 1024)
 SMEM = pl.BlockSpec(memory_space=pltpu.SMEM)
 
 
@@ -73,22 +78,15 @@
     )(clip_frames, clip_pixels, q, k, v, far_k, far_v)
 
 
-def clip_mask(cf_ref, keep_ref, frames, rolled):
-    size = keep_ref.shape[0]
+def came_from(slot, frames):
+    return lax.rem(lax.axis_index("seq") + frames - slot, frames)
+
+
+def clip_bias(cf_ref, frames):
+    size = frames * TBLOCK
     group = lax.axis_index("grp") // 2
-    me = lax.axis_index("seq")
-    row = lax.broadcasted_iota(jnp.int32, (size, size), 0)
-    col = lax.broadcasted_iota(jnp.int32, (size, size), 1)
-    same_spot = row % TBLOCK == col % TBLOCK
-
-    def frame_of(index):
-        slot = index // TBLOCK
-        if not rolled:
-            return slot
-        return (me + frames - slot) % frames
-
-    def segment_of(index):
-        frame = frame_of(index)
+
+    def segment_of(frame):
         end = 0
         segment = jnp.zeros_like(frame)
         for clip in range(CLIPS):
@@ -96,8 +94,14 @@
             segment = segment + (frame >= end).astype(jnp.int32)
         return segment
 
-    keep = same_spot & (segment_of(row) == segment_of(col))
-    keep_ref[...] = jnp.where(keep, 0.0, MASKED)
+    row = lax.broadcasted_iota(jnp.int32, (size, 1), 0)
+    col = lax.broadcasted_iota(jnp.int32, (1, size), 1)
+    row_frame = jnp.zeros_like(row)
+    for place, slot in enumerate(SLOTS):
+        row_frame = jnp.where(row // TBLOCK == place, came_from(slot, frames), row_frame)
+    same_spot = row % TBLOCK == col % TBLOCK
+    same_clip = segment_of(row_frame) == segment_of(col // TBLOCK)
+    return jnp.where(same_spot & same_clip, 0.0, MASKED)
 
 
 def temporal_block(bias, q, k, v):
@@ -108,24 +112,31 @@
     return (summed[:, :DH] / summed[:, DH:]).astype(jnp.bfloat16)
 
 
-def temporal_kernel(cf_ref, qkv_ref, o_ref, keep_ref):
-    frames, rows, width = o_ref.shape
+def temporal_kernel(cf_ref, qkv_ref, *refs):
+    outs, bias_ref = refs[:-1], refs[-1]
+    frames = len(outs)
+    rows, width = outs[0].shape
     size = frames * TBLOCK
 
     @pl.when(pl.program_id(0) == 0)
     def _():
-        clip_mask(cf_ref, keep_ref, frames, False)
-
-    bias = keep_ref[...]
+        bias_ref[...] = clip_bias(cf_ref, frames)
+
+    bias = bias_ref[...]
     for head in range(width // DH):
         lanes = pl.ds(head * DH, DH)
         for block in range(rows // TBLOCK):
-            q, k, v = (
+            at = pl.ds(block * TBLOCK, TBLOCK)
+            q = jnp.concatenate(
+                [qkv_ref[came_from(slot, frames), at, lanes] for slot in SLOTS], axis=0
+            )
+            k, v = (
                 qkv_ref[:, pl.ds(which * rows + block * TBLOCK, TBLOCK), lanes].reshape(size, DH)
-                for which in range(3)
+                for which in (1, 2)
             )
             out = temporal_block(bias, q, k, v)
-            o_ref[:, pl.ds(block * TBLOCK, TBLOCK), lanes] = out.reshape(frames, TBLOCK, DH)
+            for place, o_ref in enumerate(outs):
+                o_ref[at, lanes] = out[place * TBLOCK : (place + 1) * TBLOCK]
 
 
 def temporal_cost(frames, rows, width):
@@ -146,13 +157,42 @@
         temporal_kernel,
         grid=(width // lanes,),
         in_specs=[SMEM, pl.BlockSpec((frames, rows3, lanes), lambda h: (0, 0, h))],
-        out_specs=pl.BlockSpec((frames, rows, lanes), lambda h: (0, 0, h)),
-        out_shape=jax.ShapeDtypeStruct((frames, rows, width), jnp.bfloat16),
+        out_specs=[pl.BlockSpec((rows, lanes), lambda h: (0, h))] * frames,
+        out_shape=[jax.ShapeDtypeStruct((rows, width), jnp.bfloat16)] * frames,
         scratch_shapes=[pltpu.VMEM((size, size), jnp.float32)],
-        compiler_params=PARAMS,
+        compiler_params=WIDE,
         cost_estimate=temporal_cost(frames, rows, width),
         name="temporal",
     )(clip_frames, qkv)
+
+
+def add_kernel(frames, spatial_ref, *refs):
+    backs, o_ref = refs[:frames], refs[frames]
+    share = backs[0].shape[0]
+    for slot, back in zip(SLOTS, backs):
+        start = lax.rem(lax.axis_index("seq") + slot, frames) * share
+        at = pl.ds(pl.multiple_of(start, share), share)
+        o_ref[at, :] = (spatial_ref[at, :] + back[...].astype(jnp.float32)).astype(o_ref.dtype)
+
+
+def add_pieces(spatial, backs):
+    rows, width = spatial.shape
+    frames = len(backs)
+    share = backs[0].shape[0]
+    lanes = width // 2
+    block = pl.BlockSpec((rows, lanes), lambda h: (0, h))
+    return pl.pallas_call(
+        functools.partial(add_kernel, frames),
+        grid=(width // lanes,),
+        in_specs=[block] + [pl.BlockSpec((share, lanes), lambda h: (0, h))] * frames,
+        out_specs=block,
+        out_shape=jax.ShapeDtypeStruct((rows, width), jnp.bfloat16),
+        compiler_params=PARAMS,
+        cost_estimate=pl.CostEstimate(
+            flops=rows * width, bytes_accessed=8 * rows * width, transcendentals=0
+        ),
+        name="add_pieces",
+    )(spatial, *backs)
 
 
 def all_to_all(array):
@@ -170,9 +210,12 @@
     far_v = lax.ppermute(v, "grp", swap)
     spatial = spatial_attention(clip_frames, clip_pixels, q, k, v, far_k, far_v, 0)
     moved, spatial = lax.optimization_barrier((moved, spatial))
-    back = all_to_all(temporal_attention(clip_frames, moved, 6))
-    attended = spatial + back.reshape(rows, width).astype(jnp.float32)
-    return attended.astype(jnp.bfloat16)[None, None]
+    outs = temporal_attention(clip_frames, moved, 6)
+    backs = []
+    for slot, out in zip(SLOTS, outs):
+        pairs = [(i, (i + frames - slot) % frames) for i in range(frames)]
+        backs.append(lax.ppermute(out, "seq", pairs) if slot else out)
+    return add_pieces(spatial, backs)[None, None]
 
 
 def solution(mesh):

time: 170 us -> 168 us (0.988)
  blocking collectives: 45.1 us -> 0 us
  starting transfers between devices: 11.8 us -> 42.4 us
  waiting for transfers between devices: 79 us -> 88.1 us
  Pallas kernels: 24.1 us -> 26.7 us
    all_to_all x1 -> x0, blocking collectives: 45.1 us -> none  [all_to_all(): return lax.all_to_all(array, 'seq', split_axis=0, concat_axis=0, tiled=True)]
    ppermute x0 -> x15, starting transfers between devices: none -> 30.6 us  [on_device(): backs.append(lax.ppermute(out, 'seq', pairs) if slot else out)]
    ppermute x0 -> x15, waiting for transfers between devices: none -> 9.13 us  [on_device(): backs.append(lax.ppermute(out, 'seq', pairs) if slot else out)]
    pallas_call x0 -> x1, Pallas kernels: none -> 1.83 us  [add_pieces(): pl.pallas_call(functools.partial(add_kernel, frames), grid=(width // lane...]
    broadcast_in_dim x1 -> x0, other arithmetic: 1.7 us -> none  [on_device(): return attended.astype(jnp.bfloat16)[None, None]]
    unnamed x16 -> x20, local copies, waits for them, and re-layouts: 4.4 us -> 5.3 us
  transfers between devices with their start and end apart: 3 -> 18, of which waited for: 3 -> 12; matrix products, arithmetic and copies ran while one was open for 0% -> 0% of each run, Pallas kernels for 12% -> 12%
where the time goes in v3:
time: 168 us; the launch traced here: 167 us
  waiting for transfers between devices  88.1 us (52%)
  starting transfers between devices  42.4 us (25%)
  Pallas kernels  26.7 us (16%)
  local copies, waits for them, and re-layouts  5.3 us (3%)
  other arithmetic  3.97 us (2%)
    ppermute x1, waiting for transfers between devices, on_device(): far_k = lax.ppermute(k, 'grp', swap)  34.3 us
    ppermute x1, waiting for transfers between devices, on_device(): far_v = lax.ppermute(v, 'grp', swap)  33.7 us
    ppermute x15, starting transfers between devices, on_device(): backs.append(lax.ppermute(out, 'seq', pairs) if slot else out)  30.6 us
    pallas_call x1, Pallas kernels, spatial_attention(): pl.pallas_call(spatial_kernel, grid=(heads,), in_specs=[SMEM, SMEM, whole...  19.9 us
    all_to_all x1, waiting for transfers between devices, all_to_all(): return lax.all_to_all(array, 'seq', split_axis=0, concat_axis=0, tiled=True)  11 us
    all_to_all x1, starting transfers between devices, all_to_all(): return lax.all_to_all(array, 'seq', split_axis=0, concat_axis=0, tiled=True)  10.3 us
    ppermute x15, waiting for transfers between devices, on_device(): backs.append(lax.ppermute(out, 'seq', pairs) if slot else out)  9.13 us
    unnamed x20, local copies, waits for them, and re-layouts  5.3 us
  transfers between devices with their start and end apart: 18, of which 12 were waited for; matrix products, arithmetic and copies ran while one was open for 0% of the time, Pallas kernels for 12%

profile of v3, /device:TPU:1, one launch (start us, length us, event | category | flops | bytes accessed | tf_op | source)
XLA Modules:
  0.0 166.6 jit_solution(1505780864137211352)
XLA Ops:
  0.0 4.0 %pad_maximum_fusion = bf16[16,96,1536]{2,1,0:T(8,128)(2,1)} fusion(bf16[16,32,1536]{2,1,0:T(8,128)(2,1)} %bitcast.12, bf16[16,32,1536]{2,1,0:T(8,128)(2,1)} %bitcast.9, bf16[16,32,1536]{2,1,0:T(8,128)(2,1)} %bitcast.7), kind=kLoop, calls=%fused_computation | loop fusion | flops 14155776 | bytes 9437184 | tf_op jit(solution)/shard_map/concatenate | solution.py:207
  4.0 10.3 %all-to-all-start = ((bf16[16,96,1536]{2,1,0:T(8,128)(2,1)}), bf16[16,96,1536]{2,1,0:T(8,128)(2,1)}, u32[]{:S(2)}, u32[]{:S(2)}) async-start(bf16[16,96,1536]{2,1,0:T(8,128)(2,1)} %pad_maximum_fusion), calls=%async_computation | async-start | bytes 9437184 | tf_op jit(solution)/shard_map/all_to_all | solution.py:199
  14.3 1.3 collective-permute-start
  16.0 34.3 %collective-permute-done.fk_ref = bf16[512,1536]{1,0:T(8,128)(2,1)} collective-permute-done((bf16[512,1536]{1,0:T(8,128)(2,1)S(1)}, bf16[512,1536]{1,0:T(8,128)(2,1)}, u32[]{:S(2)}, u32[]{:S(2)}) %collective-permute-start) | collective-permute-done | bytes 1572896 | tf_op jit(solution)/shard_map/ppermute | solution.py:209
  50.3 33.7 %collective-permute-done.1.fv_ref = bf16[512,1536]{1,0:T(8,128)(2,1)} collective-permute-done((bf16[512,1536]{1,0:T(8,128)(2,1)S(1)}, bf16[512,1536]{1,0:T(8,128)(2,1)}, u32[]{:S(2)}, u32[]{:S(2)}) %collective-permute-start.1) | collective-permute-done | bytes 1572896 | tf_op jit(solution)/shard_map/ppermute | solution.py:210
  84.0 1.4 copy-done
  85.4 1.4 copy-done.2
  86.8 1.4 copy-done.4
  88.2 19.9 %spatial.1.spatial_ref = f32[512,1536]{1,0:T(8,128)S(1)} custom-call(s32[8,4]{1,0:T(8,128)S(1)} %copy.6.cf_ref, s32[8,4]{1,0:T(8,128)S(1)} %copy.7.cp_ref, bf16[512,1536]{1,0:T(8,128)(2,1)S(1)} %bitcast.8, bf16[512,1536]{1,0:T(8,128)(2,1)S(1)} %bitcast.11, bf16[512,1536]{1,0:T(8,128)(2,1)S(1)} %bitcast.14, bf16[512,1536]{1,0:T(8,128)(2,1)} %collective-permute-done.fk_ref, ...), custom_call_target="tpu_custom_call" | custom-call | flops 3221225472 | bytes 11010048 | tf_op jit(solution)/shard_map/spatial/pallas_call | solution.py:65
  108.1 11.0 %all-to-all-done.qkv_ref = bf16[16,96,1536]{2,1,0:T(8,128)(2,1)} async-done(((bf16[16,96,1536]{2,1,0:T(8,128)(2,1)}), bf16[16,96,1536]{2,1,0:T(8,128)(2,1)}, u32[]{:S(2)}, u32[]{:S(2)}) %all-to-all-start) | async-done | bytes 4718624 | tf_op jit(solution)/shard_map/all_to_all | solution.py:199
  119.1 5.0 %temporal.1 = (bf16[32,1536]{1,0:T(8,128)(2,1)}, bf16[32,1536]{1,0:T(8,128)(2,1)}, bf16[32,1536]{1,0:T(8,128)(2,1)}, bf16[32,1536]{1,0:T(8,128)(2,1)}, bf16[32,1...) custom-call(s32[8,4]{1,0:T(8,128)} %copy-done.6, ...), custom_call_target="tpu_custom_call" | custom-call | flops 805306368 | bytes 6291456 | tf_op jit(solution)/shard_map/temporal/pallas_call | solution.py:156
  124.1 3.9 %collective-permute-start.2 = (bf16[32,1536]{1,0:T(8,128)(2,1)}, bf16[32,1536]{1,0:T(8,128)(2,1)S(1)}, u32[]{:S(2)}, u32[]{:S(2)}) collective-permute-start(bf16[32,1536]{1,0:T(8,128)(2,1)} %get-tuple-element.25), channel_id=1, source_target_pairs={{0,9},{1,10},{2,11},{3,12},{4,13},{5,14},{6,15},{7,0},{8,1},{9,2},... | collective-permute-start | bytes 294920 | tf_op jit(solution)/shard_map/ppermute | solution.py:217
  128.0 1.9 %collective-permute-start.3 = (bf16[32,1536]{1,0:T(8,128)(2,1)}, bf16[32,1536]{1,0:T(8,128)(2,1)S(1)}, u32[]{:S(2)}, u32[]{:S(2)}) collective-permute-start(bf16[32,1536]{1,0:T(8,128)(2,1)} %get-tuple-element.26), channel_id=1, source_target_pairs={{0,7},{1,8},{2,9},{3,10},{4,11},{5,12},{6,13},{7,14},{8,15},{9,0},... | collective-permute-start | bytes 294920 | tf_op jit(solution)/shard_map/ppermute | solution.py:217
  129.9 3.1 %collective-permute-start.4 = (bf16[32,1536]{1,0:T(8,128)(2,1)}, bf16[32,1536]{1,0:T(8,128)(2,1)S(1)}, u32[]{:S(2)}, u32[]{:S(2)}) collective-permute-start(bf16[32,1536]{1,0:T(8,128)(2,1)} %get-tuple-element.27), channel_id=1, source_target_pairs={{0,10},{1,11},{2,12},{3,13},{4,14},{5,15},{6,0},{7,1},{8,2},{9,3},... | collective-permute-start | bytes 294920 | tf_op jit(solution)/shard_map/ppermute | solution.py:217
  133.2 3.7 %collective-permute-start.6 = (bf16[32,1536]{1,0:T(8,128)(2,1)}, bf16[32,1536]{1,0:T(8,128)(2,1)S(1)}, u32[]{:S(2)}, u32[]{:S(2)}) collective-permute-start(bf16[32,1536]{1,0:T(8,128)(2,1)} %get-tuple-element.29), channel_id=1, source_target_pairs={{0,11},{1,12},{2,13},{3,14},{4,15},{5,0},{6,1},{7,2},{8,3},{9,4},{... | collective-permute-start | bytes 294920 | tf_op jit(solution)/shard_map/ppermute | solution.py:217
  137.6 2.3 %collective-permute-done.3.refs_1_ = bf16[32,1536]{1,0:T(8,128)(2,1)S(1)} collective-permute-done((bf16[32,1536]{1,0:T(8,128)(2,1)}, bf16[32,1536]{1,0:T(8,128)(2,1)S(1)}, u32[]{:S(2)}, u32[]{:S(2)}) %collective-permute-start.3) | collective-permute-done | bytes 98336 | tf_op jit(solution)/shard_map/ppermute | solution.py:217
  139.9 3.6 %collective-permute-start.8 = (bf16[32,1536]{1,0:T(8,128)(2,1)}, bf16[32,1536]{1,0:T(8,128)(2,1)S(1)}, u32[]{:S(2)}, u32[]{:S(2)}) collective-permute-start(bf16[32,1536]{1,0:T(8,128)(2,1)} %get-tuple-element.31), channel_id=1, source_target_pairs={{0,8},{1,9},{2,10},{3,11},{4,12},{5,13},{6,14},{7,15},{8,0},{9,1},... | collective-permute-start | bytes 294920 | tf_op jit(solution)/shard_map/ppermute | solution.py:217
  143.5 1.4 collective-permute-done.4.refs_2_
  144.9 5.6 %collective-permute-start.9 = (bf16[32,1536]{1,0:T(8,128)(2,1)}, bf16[32,1536]{1,0:T(8,128)(2,1)S(1)}, u32[]{:S(2)}, u32[]{:S(2)}) collective-permute-start(bf16[32,1536]{1,0:T(8,128)(2,1)} %get-tuple-element.32), channel_id=1, source_target_pairs={{0,12},{1,13},{2,14},{3,15},{4,0},{5,1},{6,2},{7,3},{8,4},{9,5},{1... | collective-permute-start | bytes 294920 | tf_op jit(solution)/shard_map/ppermute | solution.py:217
  150.5 1.1 collective-permute-start.11
  151.6 3.7 %collective-permute-start.12 = (bf16[32,1536]{1,0:T(8,128)(2,1)}, bf16[32,1536]{1,0:T(8,128)(2,1)S(1)}, u32[]{:S(2)}, u32[]{:S(2)}) collective-permute-start(bf16[32,1536]{1,0:T(8,128)(2,1)} %get-tuple-element.35), channel_id=1, source_target_pairs={{0,3},{1,4},{2,5},{3,6},{4,7},{5,8},{6,9},{7,10},{8,11},{9,12},{10... | collective-permute-start | bytes 294920 | tf_op jit(solution)/shard_map/ppermute | solution.py:217
  155.4 1.9 %collective-permute-start.13 = (bf16[32,1536]{1,0:T(8,128)(2,1)}, bf16[32,1536]{1,0:T(8,128)(2,1)S(1)}, u32[]{:S(2)}, u32[]{:S(2)}) collective-permute-start(bf16[32,1536]{1,0:T(8,128)(2,1)} %get-tuple-element.36), channel_id=1, source_target_pairs={{0,14},{1,15},{2,0},{3,1},{4,2},{5,3},{6,4},{7,5},{8,6},{9,7},{10,... | collective-permute-start | bytes 294920 | tf_op jit(solution)/shard_map/ppermute | solution.py:217
  158.4 2.1 %collective-permute-done.11.refs_9_ = bf16[32,1536]{1,0:T(8,128)(2,1)S(1)} collective-permute-done((bf16[32,1536]{1,0:T(8,128)(2,1)}, bf16[32,1536]{1,0:T(8,128)(2,1)S(1)}, u32[]{:S(2)}, u32[]{:S(2)}) %collective-permute-start.11) | collective-permute-done | bytes 98336 | tf_op jit(solution)/shard_map/ppermute | solution.py:217
  164.8 1.8 %add_pieces.1 = bf16[512,1536]{1,0:T(8,128)(2,1)} custom-call(f32[512,1536]{1,0:T(8,128)S(1)} %spatial.1.spatial_ref, bf16[32,1536]{1,0:T(8,128)(2,1)S(1)} %collective-permute-done.2.refs_0_, bf16[32,1536]{1,0:T(8,128)(2,1)S(1)} %collective-permute-done.3.refs_1_, bf16[32,1536]{1,0:T(8,128)(2,1)S(1)} %collective-permute-done.4.refs_2_, ...), custom_call_target="tpu_custom_call" | custom-call | flops 786432 | bytes 6291456 | tf_op jit(solution)/shard_map/add_pieces/pallas_call | solution.py:184
  (36 shorter events, 6.8 us)
Async XLA Ops:
  4.0 10.3 %copy-start.1 = (bf16[1,1,512,1536]{3,2,1,0:T(8,128)(2,1)S(1)}, bf16[1,1,512,1536]{3,2,1,0:T(8,128)(2,1)}, u32[]{:S(2)}) copy-start(bf16[1,1,512,1536]{3,2,1,0:T(8,128)(2,1)} %param.6) | copy-start | bytes 4718596
  4.0 11.6 %copy-start.3 = (bf16[1,1,512,1536]{3,2,1,0:T(8,128)(2,1)S(1)}, bf16[1,1,512,1536]{3,2,1,0:T(8,128)(2,1)}, u32[]{:S(2)}) copy-start(bf16[1,1,512,1536]{3,2,1,0:T(8,128)(2,1)} %param.7) | copy-start | bytes 4718596
  4.0 11.8 %copy-start.7 = (s32[8,4]{0,1:T(4,128)S(1)}, s32[8,4]{0,1:T(4,128)}, u32[]{:S(2)}) copy-start(s32[8,4]{0,1:T(4,128)} %param.8) | copy-start | bytes 388
  4.0 11.9 %copy-start.8 = (s32[8,4]{0,1:T(4,128)S(1)}, s32[8,4]{0,1:T(4,128)}, u32[]{:S(2)}) copy-start(s32[8,4]{0,1:T(4,128)} %param.9) | copy-start | bytes 388
  4.0 115.1 %all-to-all-start = ((bf16[16,96,1536]{2,1,0:T(8,128)(2,1)}), bf16[16,96,1536]{2,1,0:T(8,128)(2,1)}, u32[]{:S(2)}, u32[]{:S(2)}) async-start(bf16[16,96,1536]{2,1,0:T(8,128)(2,1)} %pad_maximum_fusion), calls=%async_computation | async-start | bytes 9437184 | tf_op jit(solution)/shard_map/all_to_all | solution.py:199
  14.3 36.0 %collective-permute-start = (bf16[512,1536]{1,0:T(8,128)(2,1)S(1)}, bf16[512,1536]{1,0:T(8,128)(2,1)}, u32[]{:S(2)}, u32[]{:S(2)}) collective-permute-start(bf16[512,1536]{1,0:T(8,128)(2,1)S(1)} %bitcast.10), channel_id=1, source_target_pairs={{0,16},{16,0},{32,48},{48,32},{64,80},{80,64},{96,112},{112,96},{1... | collective-permute-start | bytes 4718600 | tf_op jit(solution)/shard_map/ppermute | solution.py:209
  15.6 68.4 %collective-permute-start.1 = (bf16[512,1536]{1,0:T(8,128)(2,1)S(1)}, bf16[512,1536]{1,0:T(8,128)(2,1)}, u32[]{:S(2)}, u32[]{:S(2)}) collective-permute-start(bf16[512,1536]{1,0:T(8,128)(2,1)S(1)} %bitcast.13), channel_id=1, source_target_pairs={{0,16},{16,0},{32,48},{48,32},{64,80},{80,64},{96,112},{112,96},{1... | collective-permute-start | bytes 4718600 | tf_op jit(solution)/shard_map/ppermute | solution.py:210
  15.9 92.2 %copy-start.6 = (s32[8,4]{1,0:T(8,128)}, s32[8,4]{1,0:T(8,128)S(1)}, u32[]{:S(2)}) copy-start(s32[8,4]{1,0:T(8,128)S(1)} %copy.6.cf_ref) | copy-start | bytes 388
  84.0 1.4 copy-start
  124.1 12.8 %collective-permute-start.2 = (bf16[32,1536]{1,0:T(8,128)(2,1)}, bf16[32,1536]{1,0:T(8,128)(2,1)S(1)}, u32[]{:S(2)}, u32[]{:S(2)}) collective-permute-start(bf16[32,1536]{1,0:T(8,128)(2,1)} %get-tuple-element.25), channel_id=1, source_target_pairs={{0,9},{1,10},{2,11},{3,12},{4,13},{5,14},{6,15},{7,0},{8,1},{9,2},... | collective-permute-start | bytes 294920 | tf_op jit(solution)/shard_map/ppermute | solution.py:217
  128.0 11.9 %collective-permute-start.3 = (bf16[32,1536]{1,0:T(8,128)(2,1)}, bf16[32,1536]{1,0:T(8,128)(2,1)S(1)}, u32[]{:S(2)}, u32[]{:S(2)}) collective-permute-start(bf16[32,1536]{1,0:T(8,128)(2,1)} %get-tuple-element.26), channel_id=1, source_target_pairs={{0,7},{1,8},{2,9},{3,10},{4,11},{5,12},{6,13},{7,14},{8,15},{9,0},... | collective-permute-start | bytes 294920 | tf_op jit(solution)/shard_map/ppermute | solution.py:217
  129.9 15.1 %collective-permute-start.4 = (bf16[32,1536]{1,0:T(8,128)(2,1)}, bf16[32,1536]{1,0:T(8,128)(2,1)S(1)}, u32[]{:S(2)}, u32[]{:S(2)}) collective-permute-start(bf16[32,1536]{1,0:T(8,128)(2,1)} %get-tuple-element.27), channel_id=1, source_target_pairs={{0,10},{1,11},{2,12},{3,13},{4,14},{5,15},{6,0},{7,1},{8,2},{9,3},... | collective-permute-start | bytes 294920 | tf_op jit(solution)/shard_map/ppermute | solution.py:217
  133.0 17.6 %collective-permute-start.5 = (bf16[32,1536]{1,0:T(8,128)(2,1)}, bf16[32,1536]{1,0:T(8,128)(2,1)S(1)}, u32[]{:S(2)}, u32[]{:S(2)}) collective-permute-start(bf16[32,1536]{1,0:T(8,128)(2,1)} %get-tuple-element.28), channel_id=1, source_target_pairs={{0,6},{1,7},{2,8},{3,9},{4,10},{5,11},{6,12},{7,13},{8,14},{9,15},... | collective-permute-start | bytes 294920 | tf_op jit(solution)/shard_map/ppermute | solution.py:217
  133.2 17.4 %collective-permute-start.6 = (bf16[32,1536]{1,0:T(8,128)(2,1)}, bf16[32,1536]{1,0:T(8,128)(2,1)S(1)}, u32[]{:S(2)}, u32[]{:S(2)}) collective-permute-start(bf16[32,1536]{1,0:T(8,128)(2,1)} %get-tuple-element.29), channel_id=1, source_target_pairs={{0,11},{1,12},{2,13},{3,14},{4,15},{5,0},{6,1},{7,2},{8,3},{9,4},{... | collective-permute-start | bytes 294920 | tf_op jit(solution)/shard_map/ppermute | solution.py:217
  136.9 14.8 %collective-permute-start.7 = (bf16[32,1536]{1,0:T(8,128)(2,1)}, bf16[32,1536]{1,0:T(8,128)(2,1)S(1)}, u32[]{:S(2)}, u32[]{:S(2)}) collective-permute-start(bf16[32,1536]{1,0:T(8,128)(2,1)} %get-tuple-element.30), channel_id=1, source_target_pairs={{0,5},{1,6},{2,7},{3,8},{4,9},{5,10},{6,11},{7,12},{8,13},{9,14},{... | collective-permute-start | bytes 294920 | tf_op jit(solution)/shard_map/ppermute | solution.py:217
  139.9 15.5 %collective-permute-start.8 = (bf16[32,1536]{1,0:T(8,128)(2,1)}, bf16[32,1536]{1,0:T(8,128)(2,1)S(1)}, u32[]{:S(2)}, u32[]{:S(2)}) collective-permute-start(bf16[32,1536]{1,0:T(8,128)(2,1)} %get-tuple-element.31), channel_id=1, source_target_pairs={{0,8},{1,9},{2,10},{3,11},{4,12},{5,13},{6,14},{7,15},{8,0},{9,1},... | collective-permute-start | bytes 294920 | tf_op jit(solution)/shard_map/ppermute | solution.py:217
  144.9 12.5 %collective-permute-start.9 = (bf16[32,1536]{1,0:T(8,128)(2,1)}, bf16[32,1536]{1,0:T(8,128)(2,1)S(1)}, u32[]{:S(2)}, u32[]{:S(2)}) collective-permute-start(bf16[32,1536]{1,0:T(8,128)(2,1)} %get-tuple-element.32), channel_id=1, source_target_pairs={{0,12},{1,13},{2,14},{3,15},{4,0},{5,1},{6,2},{7,3},{8,4},{9,5},{1... | collective-permute-start | bytes 294920 | tf_op jit(solution)/shard_map/ppermute | solution.py:217
  150.5 6.9 %collective-permute-start.10 = (bf16[32,1536]{1,0:T(8,128)(2,1)}, bf16[32,1536]{1,0:T(8,128)(2,1)S(1)}, u32[]{:S(2)}, u32[]{:S(2)}) collective-permute-start(bf16[32,1536]{1,0:T(8,128)(2,1)} %get-tuple-element.33), channel_id=1, source_target_pairs={{0,4},{1,5},{2,6},{3,7},{4,8},{5,9},{6,10},{7,11},{8,12},{9,13},{1... | collective-permute-start | bytes 294920 | tf_op jit(solution)/shard_map/ppermute | solution.py:217
  150.5 9.9 %collective-permute-start.11 = (bf16[32,1536]{1,0:T(8,128)(2,1)}, bf16[32,1536]{1,0:T(8,128)(2,1)S(1)}, u32[]{:S(2)}, u32[]{:S(2)}) collective-permute-start(bf16[32,1536]{1,0:T(8,128)(2,1)} %get-tuple-element.34), channel_id=1, source_target_pairs={{0,13},{1,14},{2,15},{3,0},{4,1},{5,2},{6,3},{7,4},{8,5},{9,6},{10... | collective-permute-start | bytes 294920 | tf_op jit(solution)/shard_map/ppermute | solution.py:217
  151.6 9.2 %collective-permute-start.12 = (bf16[32,1536]{1,0:T(8,128)(2,1)}, bf16[32,1536]{1,0:T(8,128)(2,1)S(1)}, u32[]{:S(2)}, u32[]{:S(2)}) collective-permute-start(bf16[32,1536]{1,0:T(8,128)(2,1)} %get-tuple-element.35), channel_id=1, source_target_pairs={{0,3},{1,4},{2,5},{3,6},{4,7},{5,8},{6,9},{7,10},{8,11},{9,12},{10... | collective-permute-start | bytes 294920 | tf_op jit(solution)/shard_map/ppermute | solution.py:217
  155.4 6.5 %collective-permute-start.13 = (bf16[32,1536]{1,0:T(8,128)(2,1)}, bf16[32,1536]{1,0:T(8,128)(2,1)S(1)}, u32[]{:S(2)}, u32[]{:S(2)}) collective-permute-start(bf16[32,1536]{1,0:T(8,128)(2,1)} %get-tuple-element.36), channel_id=1, source_target_pairs={{0,14},{1,15},{2,0},{3,1},{4,2},{5,3},{6,4},{7,5},{8,6},{9,7},{10,... | collective-permute-start | bytes 294920 | tf_op jit(solution)/shard_map/ppermute | solution.py:217
  157.4 5.6 %collective-permute-start.14 = (bf16[32,1536]{1,0:T(8,128)(2,1)}, bf16[32,1536]{1,0:T(8,128)(2,1)S(1)}, u32[]{:S(2)}, u32[]{:S(2)}) collective-permute-start(bf16[32,1536]{1,0:T(8,128)(2,1)} %get-tuple-element.37), channel_id=1, source_target_pairs={{0,2},{1,3},{2,4},{3,5},{4,6},{5,7},{6,8},{7,9},{8,10},{9,11},{10,... | collective-permute-start | bytes 294920 | tf_op jit(solution)/shard_map/ppermute | solution.py:217
  157.4 6.1 %collective-permute-start.15 = (bf16[32,1536]{1,0:T(8,128)(2,1)}, bf16[32,1536]{1,0:T(8,128)(2,1)S(1)}, u32[]{:S(2)}, u32[]{:S(2)}) collective-permute-start(bf16[32,1536]{1,0:T(8,128)(2,1)} %get-tuple-element.38), channel_id=1, source_target_pairs={{0,15},{1,0},{2,1},{3,2},{4,3},{5,4},{6,5},{7,6},{8,7},{9,8},{10,9... | collective-permute-start | bytes 294920 | tf_op jit(solution)/shard_map/ppermute | solution.py:217
  160.4 3.4 %collective-permute-start.16 = (bf16[32,1536]{1,0:T(8,128)(2,1)}, bf16[32,1536]{1,0:T(8,128)(2,1)S(1)}, u32[]{:S(2)}, u32[]{:S(2)}) collective-permute-start(bf16[32,1536]{1,0:T(8,128)(2,1)} %get-tuple-element.39), channel_id=1, source_target_pairs={{0,1},{1,2},{2,3},{3,4},{4,5},{5,6},{6,7},{7,8},{8,9},{9,10},{10,1... | collective-permute-start | bytes 294920 | tf_op jit(solution)/shard_map/ppermute | solution.py:217
  (3 other events, 3.7 us)

commit v4 on v3

--- a/solution.py
+++ b/solution.py
@@ -54,7 +54,7 @@
         total = jnp.sum(own, axis=1, keepdims=True) + jnp.sum(far, axis=1, keepdims=True)
         summed = product(own.astype(jnp.bfloat16), v_ref[:, lanes])
         summed = summed + product(far.astype(jnp.bfloat16), fv_ref[:, lanes])
-        o_ref[:, lanes] = summed / total
+        o_ref[:, lanes] = (summed / total).astype(o_ref.dtype)
 
 
 def spatial_attention(clip_frames, clip_pixels, q, k, v, far_k, far_v, start):
@@ -67,7 +67,7 @@
         grid=(heads,),
         in_specs=[SMEM, SMEM, whole, whole, whole, block, block],
         out_specs=block,
-        out_shape=jax.ShapeDtypeStruct((rows, width), jnp.float32),
+        out_shape=jax.ShapeDtypeStruct((rows, width), jnp.bfloat16),
         compiler_params=PARAMS,
         cost_estimate=pl.CostEstimate(
             flops=8 * rows * rows * width,
@@ -172,7 +172,8 @@
     for slot, back in zip(SLOTS, backs):
         start = lax.rem(lax.axis_index("seq") + slot, frames) * share
         at = pl.ds(pl.multiple_of(start, share), share)
-        o_ref[at, :] = (spatial_ref[at, :] + back[...].astype(jnp.float32)).astype(o_ref.dtype)
+        both = spatial_ref[at, :].astype(jnp.float32) + back[...].astype(jnp.float32)
+        o_ref[at, :] = both.astype(o_ref.dtype)
 
 
 def add_pieces(spatial, backs):

time: 168 us -> 168 us (level)
  waiting for transfers between devices: 88.1 us -> 89.9 us
    all_to_all x1, waiting for transfers between devices: 11 us -> 12.7 us  [all_to_all(): return lax.all_to_all(array, 'seq', split_axis=0, concat_axis=0, tiled=True)]
where the time goes in v4:
time: 168 us; the launch traced here: 167 us
  waiting for transfers between devices  89.9 us (54%)
  starting transfers between devices  42.4 us (25%)
  Pallas kernels  26.8 us (16%)
  other arithmetic  3.97 us (2%)
  local copies, waits for them, and re-layouts  3.62 us (2%)
    ppermute x1, waiting for transfers between devices, on_device(): far_k = lax.ppermute(k, 'grp', swap)  34.3 us
    ppermute x1, waiting for transfers between devices, on_device(): far_v = lax.ppermute(v, 'grp', swap)  33.7 us
    ppermute x15, starting transfers between devices, on_device(): backs.append(lax.ppermute(out, 'seq', pairs) if slot else out)  30.6 us
    pallas_call x1, Pallas kernels, spatial_attention(): pl.pallas_call(spatial_kernel, grid=(heads,), in_specs=[SMEM, SMEM, whole...  19.8 us
    all_to_all x1, waiting for transfers between devices, all_to_all(): return lax.all_to_all(array, 'seq', split_axis=0, concat_axis=0, tiled=True)  12.7 us
    all_to_all x1, starting transfers between devices, all_to_all(): return lax.all_to_all(array, 'seq', split_axis=0, concat_axis=0, tiled=True)  10.3 us
    ppermute x15, waiting for transfers between devices, on_device(): backs.append(lax.ppermute(out, 'seq', pairs) if slot else out)  9.18 us
    pallas_call x1, Pallas kernels, temporal_attention(): pl.pallas_call(temporal_kernel, grid=(width // lanes,), in_specs=[SMEM, p...  5.23 us
  transfers between devices with their start and end apart: 18, of which 12 were waited for; matrix products, arithmetic and copies ran while one was open for 0% of the time, Pallas kernels for 12%

profile of v4, /device:TPU:1, one launch (start us, length us, event | category | flops | bytes accessed | tf_op | source)
XLA Modules:
  0.0 166.7 jit_solution(5472124751172762165)
XLA Ops:
  0.0 4.0 %pad_maximum_fusion = bf16[16,96,1536]{2,1,0:T(8,128)(2,1)} fusion(bf16[16,32,1536]{2,1,0:T(8,128)(2,1)} %bitcast.12, bf16[16,32,1536]{2,1,0:T(8,128)(2,1)} %bitcast.9, bf16[16,32,1536]{2,1,0:T(8,128)(2,1)} %bitcast.7), kind=kLoop, calls=%fused_computation | loop fusion | flops 14155776 | bytes 9437184 | tf_op jit(solution)/shard_map/concatenate | solution.py:208
  4.0 10.3 %all-to-all-start = ((bf16[16,96,1536]{2,1,0:T(8,128)(2,1)}), bf16[16,96,1536]{2,1,0:T(8,128)(2,1)}, u32[]{:S(2)}, u32[]{:S(2)}) async-start(bf16[16,96,1536]{2,1,0:T(8,128)(2,1)} %pad_maximum_fusion), calls=%async_computation | async-start | bytes 9437184 | tf_op jit(solution)/shard_map/all_to_all | solution.py:200
  14.3 1.3 collective-permute-start
  16.0 34.3 %collective-permute-done.fk_ref = bf16[512,1536]{1,0:T(8,128)(2,1)} collective-permute-done((bf16[512,1536]{1,0:T(8,128)(2,1)S(1)}, bf16[512,1536]{1,0:T(8,128)(2,1)}, u32[]{:S(2)}, u32[]{:S(2)}) %collective-permute-start) | collective-permute-done | bytes 1572896 | tf_op jit(solution)/shard_map/ppermute | solution.py:210
  50.3 33.7 %collective-permute-done.1.fv_ref = bf16[512,1536]{1,0:T(8,128)(2,1)} collective-permute-done((bf16[512,1536]{1,0:T(8,128)(2,1)}, bf16[512,1536]{1,0:T(8,128)(2,1)}, u32[]{:S(2)}, u32[]{:S(2)}) %collective-permute-start.1) | collective-permute-done | bytes 1572896 | tf_op jit(solution)/shard_map/ppermute | solution.py:211
  84.0 1.4 copy-done.2
  85.4 19.8 %spatial.1.spatial_ref = bf16[512,1536]{1,0:T(8,128)(2,1)S(1)} custom-call(s32[8,4]{1,0:T(8,128)S(1)} %copy.6.cf_ref, s32[8,4]{1,0:T(8,128)S(1)} %copy.7.cp_ref, bf16[512,1536]{1,0:T(8,128)(2,1)S(1)} %bitcast.8, bf16[512,1536]{1,0:T(8,128)(2,1)S(1)} %bitcast.11, bf16[512,1536]{1,0:T(8,128)(2,1)S(1)} %bitcast.14, ...), custom_call_target="tpu_custom_call" | custom-call | flops 3221225472 | bytes 11010048 | tf_op jit(solution)/shard_map/spatial/pallas_call | solution.py:65
  105.3 1.1 copy-done.3
  106.4 12.7 %all-to-all-done.qkv_ref = bf16[16,96,1536]{2,1,0:T(8,128)(2,1)} async-done(((bf16[16,96,1536]{2,1,0:T(8,128)(2,1)}), bf16[16,96,1536]{2,1,0:T(8,128)(2,1)}, u32[]{:S(2)}, u32[]{:S(2)}) %all-to-all-start) | async-done | bytes 4718624 | tf_op jit(solution)/shard_map/all_to_all | solution.py:200
  119.1 5.2 %temporal.1 = (bf16[32,1536]{1,0:T(8,128)(2,1)}, bf16[32,1536]{1,0:T(8,128)(2,1)}, bf16[32,1536]{1,0:T(8,128)(2,1)}, bf16[32,1536]{1,0:T(8,128)(2,1)}, bf16[32,1...) custom-call(s32[8,4]{1,0:T(8,128)} %copy-done.6, ...), custom_call_target="tpu_custom_call" | custom-call | flops 805306368 | bytes 6291456 | tf_op jit(solution)/shard_map/temporal/pallas_call | solution.py:156
  124.3 3.9 %collective-permute-start.2 = (bf16[32,1536]{1,0:T(8,128)(2,1)}, bf16[32,1536]{1,0:T(8,128)(2,1)S(1)}, u32[]{:S(2)}, u32[]{:S(2)}) collective-permute-start(bf16[32,1536]{1,0:T(8,128)(2,1)} %get-tuple-element.25), channel_id=1, source_target_pairs={{0,9},{1,10},{2,11},{3,12},{4,13},{5,14},{6,15},{7,0},{8,1},{9,2},... | collective-permute-start | bytes 294920 | tf_op jit(solution)/shard_map/ppermute | solution.py:218
  128.2 1.9 %collective-permute-start.3 = (bf16[32,1536]{1,0:T(8,128)(2,1)}, bf16[32,1536]{1,0:T(8,128)(2,1)S(1)}, u32[]{:S(2)}, u32[]{:S(2)}) collective-permute-start(bf16[32,1536]{1,0:T(8,128)(2,1)} %get-tuple-element.26), channel_id=1, source_target_pairs={{0,7},{1,8},{2,9},{3,10},{4,11},{5,12},{6,13},{7,14},{8,15},{9,0},... | collective-permute-start | bytes 294920 | tf_op jit(solution)/shard_map/ppermute | solution.py:218
  130.1 3.1 %collective-permute-start.4 = (bf16[32,1536]{1,0:T(8,128)(2,1)}, bf16[32,1536]{1,0:T(8,128)(2,1)S(1)}, u32[]{:S(2)}, u32[]{:S(2)}) collective-permute-start(bf16[32,1536]{1,0:T(8,128)(2,1)} %get-tuple-element.27), channel_id=1, source_target_pairs={{0,10},{1,11},{2,12},{3,13},{4,14},{5,15},{6,0},{7,1},{8,2},{9,3},... | collective-permute-start | bytes 294920 | tf_op jit(solution)/shard_map/ppermute | solution.py:218
  133.4 3.7 %collective-permute-start.6 = (bf16[32,1536]{1,0:T(8,128)(2,1)}, bf16[32,1536]{1,0:T(8,128)(2,1)S(1)}, u32[]{:S(2)}, u32[]{:S(2)}) collective-permute-start(bf16[32,1536]{1,0:T(8,128)(2,1)} %get-tuple-element.29), channel_id=1, source_target_pairs={{0,11},{1,12},{2,13},{3,14},{4,15},{5,0},{6,1},{7,2},{8,3},{9,4},{... | collective-permute-start | bytes 294920 | tf_op jit(solution)/shard_map/ppermute | solution.py:218
  137.8 2.3 %collective-permute-done.3.refs_1_ = bf16[32,1536]{1,0:T(8,128)(2,1)S(1)} collective-permute-done((bf16[32,1536]{1,0:T(8,128)(2,1)}, bf16[32,1536]{1,0:T(8,128)(2,1)S(1)}, u32[]{:S(2)}, u32[]{:S(2)}) %collective-permute-start.3) | collective-permute-done | bytes 98336 | tf_op jit(solution)/shard_map/ppermute | solution.py:218
  140.1 3.7 %collective-permute-start.8 = (bf16[32,1536]{1,0:T(8,128)(2,1)}, bf16[32,1536]{1,0:T(8,128)(2,1)S(1)}, u32[]{:S(2)}, u32[]{:S(2)}) collective-permute-start(bf16[32,1536]{1,0:T(8,128)(2,1)} %get-tuple-element.31), channel_id=1, source_target_pairs={{0,8},{1,9},{2,10},{3,11},{4,12},{5,13},{6,14},{7,15},{8,0},{9,1},... | collective-permute-start | bytes 294920 | tf_op jit(solution)/shard_map/ppermute | solution.py:218
  143.8 1.3 collective-permute-done.4.refs_2_
  145.0 5.7 %collective-permute-start.9 = (bf16[32,1536]{1,0:T(8,128)(2,1)}, bf16[32,1536]{1,0:T(8,128)(2,1)S(1)}, u32[]{:S(2)}, u32[]{:S(2)}) collective-permute-start(bf16[32,1536]{1,0:T(8,128)(2,1)} %get-tuple-element.32), channel_id=1, source_target_pairs={{0,12},{1,13},{2,14},{3,15},{4,0},{5,1},{6,2},{7,3},{8,4},{9,5},{1... | collective-permute-start | bytes 294920 | tf_op jit(solution)/shard_map/ppermute | solution.py:218
  150.7 1.2 collective-permute-start.11
  151.9 3.7 %collective-permute-start.12 = (bf16[32,1536]{1,0:T(8,128)(2,1)}, bf16[32,1536]{1,0:T(8,128)(2,1)S(1)}, u32[]{:S(2)}, u32[]{:S(2)}) collective-permute-start(bf16[32,1536]{1,0:T(8,128)(2,1)} %get-tuple-element.35), channel_id=1, source_target_pairs={{0,3},{1,4},{2,5},{3,6},{4,7},{5,8},{6,9},{7,10},{8,11},{9,12},{10... | collective-permute-start | bytes 294920 | tf_op jit(solution)/shard_map/ppermute | solution.py:218
  155.6 1.6 collective-permute-start.13
  158.8 1.9 %collective-permute-done.11.refs_9_ = bf16[32,1536]{1,0:T(8,128)(2,1)S(1)} collective-permute-done((bf16[32,1536]{1,0:T(8,128)(2,1)}, bf16[32,1536]{1,0:T(8,128)(2,1)S(1)}, u32[]{:S(2)}, u32[]{:S(2)}) %collective-permute-start.11) | collective-permute-done | bytes 98336 | tf_op jit(solution)/shard_map/ppermute | solution.py:218
  161.9 1.2 collective-permute-done.14.refs_12_
  165.0 1.8 %add_pieces.1 = bf16[512,1536]{1,0:T(8,128)(2,1)} custom-call(bf16[512,1536]{1,0:T(8,128)(2,1)S(1)} %copy-done.4, bf16[32,1536]{1,0:T(8,128)(2,1)S(1)} %collective-permute-done.2.refs_0_, bf16[32,1536]{1,0:T(8,128)(2,1)S(1)} %collective-permute-done.3.refs_1_, bf16[32,1536]{1,0:T(8,128)(2,1)S(1)} %collective-permute-done.4.refs_2_, ...), custom_call_target="tpu_custom_call" | custom-call | flops 786432 | bytes 6291456 | tf_op jit(solution)/shard_map/add_pieces/pallas_call | solution.py:185
  (36 shorter events, 6.1 us)
Async XLA Ops:
  4.0 10.3 %copy-start.1 = (bf16[1,1,512,1536]{3,2,1,0:T(8,128)(2,1)S(1)}, bf16[1,1,512,1536]{3,2,1,0:T(8,128)(2,1)}, u32[]{:S(2)}) copy-start(bf16[1,1,512,1536]{3,2,1,0:T(8,128)(2,1)} %param.6) | copy-start | bytes 4718596
  4.0 11.8 %copy-start.7 = (s32[8,4]{0,1:T(4,128)S(1)}, s32[8,4]{0,1:T(4,128)}, u32[]{:S(2)}) copy-start(s32[8,4]{0,1:T(4,128)} %param.8) | copy-start | bytes 388
  4.0 11.9 %copy-start.8 = (s32[8,4]{0,1:T(4,128)S(1)}, s32[8,4]{0,1:T(4,128)}, u32[]{:S(2)}) copy-start(s32[8,4]{0,1:T(4,128)} %param.9) | copy-start | bytes 388
  4.0 80.0 %copy-start = (bf16[1,1,512,1536]{3,2,1,0:T(8,128)(2,1)S(1)}, bf16[1,1,512,1536]{3,2,1,0:T(8,128)(2,1)}, u32[]{:S(2)}) copy-start(bf16[1,1,512,1536]{3,2,1,0:T(8,128)(2,1)} %param.5) | copy-start | bytes 4718596
  4.0 115.1 %all-to-all-start = ((bf16[16,96,1536]{2,1,0:T(8,128)(2,1)}), bf16[16,96,1536]{2,1,0:T(8,128)(2,1)}, u32[]{:S(2)}, u32[]{:S(2)}) async-start(bf16[16,96,1536]{2,1,0:T(8,128)(2,1)} %pad_maximum_fusion), calls=%async_computation | async-start | bytes 9437184 | tf_op jit(solution)/shard_map/all_to_all | solution.py:200
  14.3 36.0 %collective-permute-start = (bf16[512,1536]{1,0:T(8,128)(2,1)S(1)}, bf16[512,1536]{1,0:T(8,128)(2,1)}, u32[]{:S(2)}, u32[]{:S(2)}) collective-permute-start(bf16[512,1536]{1,0:T(8,128)(2,1)S(1)} %bitcast.10), channel_id=1, source_target_pairs={{0,16},{16,0},{32,48},{48,32},{64,80},{80,64},{96,112},{112,96},{1... | collective-permute-start | bytes 4718600 | tf_op jit(solution)/shard_map/ppermute | solution.py:210
  15.6 68.4 %collective-permute-start.1 = (bf16[512,1536]{1,0:T(8,128)(2,1)}, bf16[512,1536]{1,0:T(8,128)(2,1)}, u32[]{:S(2)}, u32[]{:S(2)}) collective-permute-start(bf16[512,1536]{1,0:T(8,128)(2,1)} %bitcast.13), channel_id=1, source_target_pairs={{0,16},{16,0},{32,48},{48,32},{64,80},{80,64},{96,112},{112,96},{1... | collective-permute-start | bytes 4718600 | tf_op jit(solution)/shard_map/ppermute | solution.py:211
  15.9 89.4 %copy-start.6 = (s32[8,4]{1,0:T(8,128)}, s32[8,4]{1,0:T(8,128)S(1)}, u32[]{:S(2)}) copy-start(s32[8,4]{1,0:T(8,128)S(1)} %copy.6.cf_ref) | copy-start | bytes 388
  119.1 45.0 %copy-start.4 = (bf16[512,1536]{1,0:T(8,128)(2,1)S(1)}, bf16[512,1536]{1,0:T(8,128)(2,1)}, u32[]{:S(2)}) copy-start(bf16[512,1536]{1,0:T(8,128)(2,1)} %copy-done.3) | copy-start | bytes 4718596
  124.3 12.8 %collective-permute-start.2 = (bf16[32,1536]{1,0:T(8,128)(2,1)}, bf16[32,1536]{1,0:T(8,128)(2,1)S(1)}, u32[]{:S(2)}, u32[]{:S(2)}) collective-permute-start(bf16[32,1536]{1,0:T(8,128)(2,1)} %get-tuple-element.25), channel_id=1, source_target_pairs={{0,9},{1,10},{2,11},{3,12},{4,13},{5,14},{6,15},{7,0},{8,1},{9,2},... | collective-permute-start | bytes 294920 | tf_op jit(solution)/shard_map/ppermute | solution.py:218
  128.2 11.9 %collective-permute-start.3 = (bf16[32,1536]{1,0:T(8,128)(2,1)}, bf16[32,1536]{1,0:T(8,128)(2,1)S(1)}, u32[]{:S(2)}, u32[]{:S(2)}) collective-permute-start(bf16[32,1536]{1,0:T(8,128)(2,1)} %get-tuple-element.26), channel_id=1, source_target_pairs={{0,7},{1,8},{2,9},{3,10},{4,11},{5,12},{6,13},{7,14},{8,15},{9,0},... | collective-permute-start | bytes 294920 | tf_op jit(solution)/shard_map/ppermute | solution.py:218
  130.1 15.0 %collective-permute-start.4 = (bf16[32,1536]{1,0:T(8,128)(2,1)}, bf16[32,1536]{1,0:T(8,128)(2,1)S(1)}, u32[]{:S(2)}, u32[]{:S(2)}) collective-permute-start(bf16[32,1536]{1,0:T(8,128)(2,1)} %get-tuple-element.27), channel_id=1, source_target_pairs={{0,10},{1,11},{2,12},{3,13},{4,14},{5,15},{6,0},{7,1},{8,2},{9,3},... | collective-permute-start | bytes 294920 | tf_op jit(solution)/shard_map/ppermute | solution.py:218
  133.2 17.6 %collective-permute-start.5 = (bf16[32,1536]{1,0:T(8,128)(2,1)}, bf16[32,1536]{1,0:T(8,128)(2,1)S(1)}, u32[]{:S(2)}, u32[]{:S(2)}) collective-permute-start(bf16[32,1536]{1,0:T(8,128)(2,1)} %get-tuple-element.28), channel_id=1, source_target_pairs={{0,6},{1,7},{2,8},{3,9},{4,10},{5,11},{6,12},{7,13},{8,14},{9,15},... | collective-permute-start | bytes 294920 | tf_op jit(solution)/shard_map/ppermute | solution.py:218
  133.4 17.4 %collective-permute-start.6 = (bf16[32,1536]{1,0:T(8,128)(2,1)}, bf16[32,1536]{1,0:T(8,128)(2,1)S(1)}, u32[]{:S(2)}, u32[]{:S(2)}) collective-permute-start(bf16[32,1536]{1,0:T(8,128)(2,1)} %get-tuple-element.29), channel_id=1, source_target_pairs={{0,11},{1,12},{2,13},{3,14},{4,15},{5,0},{6,1},{7,2},{8,3},{9,4},{... | collective-permute-start | bytes 294920 | tf_op jit(solution)/shard_map/ppermute | solution.py:218
  137.1 14.8 %collective-permute-start.7 = (bf16[32,1536]{1,0:T(8,128)(2,1)}, bf16[32,1536]{1,0:T(8,128)(2,1)S(1)}, u32[]{:S(2)}, u32[]{:S(2)}) collective-permute-start(bf16[32,1536]{1,0:T(8,128)(2,1)} %get-tuple-element.30), channel_id=1, source_target_pairs={{0,5},{1,6},{2,7},{3,8},{4,9},{5,10},{6,11},{7,12},{8,13},{9,14},{... | collective-permute-start | bytes 294920 | tf_op jit(solution)/shard_map/ppermute | solution.py:218
  140.1 15.5 %collective-permute-start.8 = (bf16[32,1536]{1,0:T(8,128)(2,1)}, bf16[32,1536]{1,0:T(8,128)(2,1)S(1)}, u32[]{:S(2)}, u32[]{:S(2)}) collective-permute-start(bf16[32,1536]{1,0:T(8,128)(2,1)} %get-tuple-element.31), channel_id=1, source_target_pairs={{0,8},{1,9},{2,10},{3,11},{4,12},{5,13},{6,14},{7,15},{8,0},{9,1},... | collective-permute-start | bytes 294920 | tf_op jit(solution)/shard_map/ppermute | solution.py:218
  145.0 12.8 %collective-permute-start.9 = (bf16[32,1536]{1,0:T(8,128)(2,1)}, bf16[32,1536]{1,0:T(8,128)(2,1)S(1)}, u32[]{:S(2)}, u32[]{:S(2)}) collective-permute-start(bf16[32,1536]{1,0:T(8,128)(2,1)} %get-tuple-element.32), channel_id=1, source_target_pairs={{0,12},{1,13},{2,14},{3,15},{4,0},{5,1},{6,2},{7,3},{8,4},{9,5},{1... | collective-permute-start | bytes 294920 | tf_op jit(solution)/shard_map/ppermute | solution.py:218
  150.7 7.1 %collective-permute-start.10 = (bf16[32,1536]{1,0:T(8,128)(2,1)}, bf16[32,1536]{1,0:T(8,128)(2,1)S(1)}, u32[]{:S(2)}, u32[]{:S(2)}) collective-permute-start(bf16[32,1536]{1,0:T(8,128)(2,1)} %get-tuple-element.33), channel_id=1, source_target_pairs={{0,4},{1,5},{2,6},{3,7},{4,8},{5,9},{6,10},{7,11},{8,12},{9,13},{1... | collective-permute-start | bytes 294920 | tf_op jit(solution)/shard_map/ppermute | solution.py:218
  150.7 9.9 %collective-permute-start.11 = (bf16[32,1536]{1,0:T(8,128)(2,1)}, bf16[32,1536]{1,0:T(8,128)(2,1)S(1)}, u32[]{:S(2)}, u32[]{:S(2)}) collective-permute-start(bf16[32,1536]{1,0:T(8,128)(2,1)} %get-tuple-element.34), channel_id=1, source_target_pairs={{0,13},{1,14},{2,15},{3,0},{4,1},{5,2},{6,3},{7,4},{8,5},{9,6},{10... | collective-permute-start | bytes 294920 | tf_op jit(solution)/shard_map/ppermute | solution.py:218
  151.9 9.3 %collective-permute-start.12 = (bf16[32,1536]{1,0:T(8,128)(2,1)}, bf16[32,1536]{1,0:T(8,128)(2,1)S(1)}, u32[]{:S(2)}, u32[]{:S(2)}) collective-permute-start(bf16[32,1536]{1,0:T(8,128)(2,1)} %get-tuple-element.35), channel_id=1, source_target_pairs={{0,3},{1,4},{2,5},{3,6},{4,7},{5,8},{6,9},{7,10},{8,11},{9,12},{10... | collective-permute-start | bytes 294920 | tf_op jit(solution)/shard_map/ppermute | solution.py:218
  155.6 6.3 %collective-permute-start.13 = (bf16[32,1536]{1,0:T(8,128)(2,1)}, bf16[32,1536]{1,0:T(8,128)(2,1)S(1)}, u32[]{:S(2)}, u32[]{:S(2)}) collective-permute-start(bf16[32,1536]{1,0:T(8,128)(2,1)} %get-tuple-element.36), channel_id=1, source_target_pairs={{0,14},{1,15},{2,0},{3,1},{4,2},{5,3},{6,4},{7,5},{8,6},{9,7},{10,... | collective-permute-start | bytes 294920 | tf_op jit(solution)/shard_map/ppermute | solution.py:218
  157.8 5.3 %collective-permute-start.14 = (bf16[32,1536]{1,0:T(8,128)(2,1)}, bf16[32,1536]{1,0:T(8,128)(2,1)S(1)}, u32[]{:S(2)}, u32[]{:S(2)}) collective-permute-start(bf16[32,1536]{1,0:T(8,128)(2,1)} %get-tuple-element.37), channel_id=1, source_target_pairs={{0,2},{1,3},{2,4},{3,5},{4,6},{5,7},{6,8},{7,9},{8,10},{9,11},{10,... | collective-permute-start | bytes 294920 | tf_op jit(solution)/shard_map/ppermute | solution.py:218
  157.8 5.9 %collective-permute-start.15 = (bf16[32,1536]{1,0:T(8,128)(2,1)}, bf16[32,1536]{1,0:T(8,128)(2,1)S(1)}, u32[]{:S(2)}, u32[]{:S(2)}) collective-permute-start(bf16[32,1536]{1,0:T(8,128)(2,1)} %get-tuple-element.38), channel_id=1, source_target_pairs={{0,15},{1,0},{2,1},{3,2},{4,3},{5,4},{6,5},{7,6},{8,7},{9,8},{10,9... | collective-permute-start | bytes 294920 | tf_op jit(solution)/shard_map/ppermute | solution.py:218
  160.7 3.4 %collective-permute-start.16 = (bf16[32,1536]{1,0:T(8,128)(2,1)}, bf16[32,1536]{1,0:T(8,128)(2,1)S(1)}, u32[]{:S(2)}, u32[]{:S(2)}) collective-permute-start(bf16[32,1536]{1,0:T(8,128)(2,1)} %get-tuple-element.39), channel_id=1, source_target_pairs={{0,1},{1,2},{2,3},{3,4},{4,5},{5,6},{6,7},{7,8},{8,9},{9,10},{10,1... | collective-permute-start | bytes 294920 | tf_op jit(solution)/shard_map/ppermute | solution.py:218
  (3 other events, 3.4 us)
